TPU v7x, 512 devices: a whole 4x4x16 slice. The times are simulated.
512 devices in a mesh: samp: 8 (over x, core), field: 64 (over y, z).
Axes of the slice: x: 4, y: 4, z: 16, core: 2. Of those that a mesh axis runs over, the one named last changes fastest.
Arguments:
- mean_start: float32 [128, 128, 256], P('field'), may hold values from -3 to 3
- sample_draws: float32 [4, 128, 128, 256], P(None, 'field'), may hold values from -3 to 3
- kernel: float32 [3, 256], replicated, may hold values from 0.15 to 0.35
- sight_mask: int32 [128, 128], P('field'), may hold values 0 or 1
- noise_weight: float32 [128, 128], P('field'), may hold values from 0.2 to 5
- data: float32 [128, 128], P('field'), may hold values from 0.6 to 1.6
Outputs:
- mean_final: float32 [128, 128, 256], P('field')
- cg_residual: float32 [128, 128, 256], P('field')
All inputs are finite; a program needn't handle non-finite values. No bound on the sum of `sight_mask` on one device may be relied on, other than what follows from the above.
Results may differ from a plain program's by a relative error of at most 0.0065.
Values sent between devices are 32-bit elements; how exact they have to be, the bound alone decides.
No kernel may reach another device: no remote copies, remote signals or barrier semaphores. Data moves between devices by JAX's collectives and lax.ppermute only.
A program may use at most 64 MiB of HBM per device.

v0:
```python
import jax
import jax.numpy as jnp
from jax import lax
from jax.sharding import PartitionSpec as P

NEWTON = 2
ITERS = 3


def padded_2(cells, sides, width):
    for axis, dim in sides:
        count = lax.axis_size(axis)
        ends = count - 1
        head = lax.slice_in_dim(cells, 0, width, axis=dim)
        tail = lax.slice_in_dim(cells, cells.shape[dim] - width, cells.shape[dim], axis=dim)
        cells = jnp.concatenate(
            [
                lax.ppermute(tail, axis, [(i, (i + 1) % count) for i in range(ends)]),
                cells,
                lax.ppermute(head, axis, [((i + 1) % count, i) for i in range(ends)]),
            ],
            axis=dim,
        )
    return cells


def refine(v, kernel):
    padded = padded_2(v, (("field", 0),), 1)
    return kernel[0] * padded[:-2] + kernel[1] * padded[1:-1] + kernel[2] * padded[2:]


def average_back(term, kernel, count):
    summed = lax.psum(term, "samp")
    padded = padded_2(summed, (("field", 0),), 1)
    return (kernel[0] * padded[2:] + kernel[1] * padded[1:-1] + kernel[2] * padded[:-2]) / count


def squares(residual):
    return lax.psum(jnp.sum(residual * residual), "field")


def inner_product(direction, image):
    return lax.psum(jnp.sum(direction * image), "field")


def local(mean_start, sample_draws, kernel, sight_mask, noise_weight, data):
    count = lax.axis_size("samp")
    depth = mean_start.shape[2]
    scale_q = 1.0 / jnp.sqrt(jnp.float32(depth))
    member = lax.axis_index("samp")
    sign = 1.0 - 2.0 * (member % 2).astype(jnp.float32)
    latent_draw = sign * lax.dynamic_index_in_dim(sample_draws, member // 2, 0, keepdims=False)
    latent = mean_start
    maskf = sight_mask.astype(jnp.float32)
    residual = latent
    weight_col = maskf * noise_weight * scale_q * scale_q
    for outer in range(NEWTON):
        signal = jnp.exp(refine(latent + latent_draw, kernel))
        error = scale_q * (maskf * jnp.sum(signal, axis=2) - depth * data)
        gradient = latent + average_back(
            signal * (maskf * noise_weight * error * scale_q)[:, :, None], kernel, count
        )

        def metric(v, signal=signal):
            column = jnp.sum(signal * refine(v, kernel), axis=2)
            return v + average_back(signal * (weight_col * column)[:, :, None], kernel, count)

        step = jnp.zeros_like(latent)
        residual = -gradient
        direction = residual
        norm_now = squares(residual)
        for inner in range(ITERS):
            image = metric(direction)
            alpha = norm_now / inner_product(direction, image)
            step = step + alpha * direction
            residual = residual - alpha * image
            norm_next = squares(residual)
            direction = residual + norm_next / norm_now * direction
            norm_now = norm_next
        latent = latent + step
    return (latent, residual)


def solution(mesh):
    placed = (
        P("field", None, None),
        P(None, "field", None, None),
        P(),
        P("field", None),
        P("field", None),
        P("field", None),
    )
    return jax.shard_map(
        local,
        mesh=mesh,
        in_specs=placed,
        out_specs=(P("field", None, None), P("field", None, None)),
        check_vma=False,
    )
```

profile of v0, /device:TPU:1, one launch (start us, length us, event | category | flops | bytes accessed | tf_op | source)
XLA Modules:
  0.0 2158.8 jit_solution(2932000134697140681)
XLA Ops:
  8.3 4.4 collective-permute-start
  14.7 4.0 collective-permute-done.1
  20.4 79.4 %all-reduce.11.cloned.1.call-done = f32[2,128,256]{2,1,0:T(8,128)} async-done(((f32[2,128,256]{2,1,0:T(8,128)}), f32[2,128,256]{2,1,0:T(8,128)}) %all-reduce.11.cloned.1.call-update) | async-done | bytes 262160 | tf_op jit(solution)/shard_map/psum | solution.py:33
  102.1 4.0 collective-permute-start.3
  106.5 1.5 collective-permute-done.3
  108.2 4.1 collective-permute-start.4
  114.2 3.8 collective-permute-done.5
  119.0 79.0 %all-reduce.13.cloned.1.call-done = f32[2,128,256]{2,1,0:T(8,128)} async-done(((f32[2,128,256]{2,1,0:T(8,128)}), f32[2,128,256]{2,1,0:T(8,128)}) %all-reduce.13.cloned.1.call-update) | async-done | bytes 262160 | tf_op jit(solution)/shard_map/psum | solution.py:33
  200.3 4.0 collective-permute-start.7
  204.7 1.5 collective-permute-done.7
  207.0 118.3 %all-reduce.1 = (f32[]{:T(128)}, f32[]{:T(128)}) all-reduce(f32[]{:T(128)} %get-tuple-element.5, f32[]{:T(128)} %get-tuple-element.4), channel_id=1, replica_groups=mesh['samp'=8,'field'=64] {'field'}, use_global_device_ids=true, to_apply=%region_3.4 | all-reduce | flops 2 | bytes 16 | tf_op jit(solution)/shard_map/psum | solution.py:39
  327.4 111.0 %psum.144 = f32[]{:T(128)} all-reduce(f32[]{:T(128)} %get-tuple-element.21), channel_id=1, replica_groups=mesh['samp'=8,'field'=64] {'field'}, use_global_device_ids=true, to_apply=%region_9.10 | all-reduce | flops 1 | bytes 8 | tf_op jit(solution)/shard_map/psum | solution.py:39
  439.7 3.5 collective-permute-start.8
  445.2 3.8 collective-permute-done.9
  450.1 121.6 %all-reduce.15.cloned.1.call-done = f32[2,128,256]{2,1,0:T(8,128)} async-done(((f32[2,128,256]{2,1,0:T(8,128)}), f32[2,128,256]{2,1,0:T(8,128)}) %all-reduce.15.cloned.1.call-update) | async-done | bytes 262160 | tf_op jit(solution)/shard_map/psum | solution.py:33
  574.0 4.0 collective-permute-start.11
  580.6 118.3 %psum.146 = f32[]{:T(128)} all-reduce(f32[]{:T(128)} %get-tuple-element.19), channel_id=1, replica_groups=mesh['samp'=8,'field'=64] {'field'}, use_global_device_ids=true, to_apply=%region_13.14 | all-reduce | flops 1 | bytes 8 | tf_op jit(solution)/shard_map/psum | solution.py:43
  700.9 110.9 %psum.147 = f32[]{:T(128)} all-reduce(f32[]{:T(128)} %multiply_reduce_fusion.6), channel_id=1, replica_groups=mesh['samp'=8,'field'=64] {'field'}, use_global_device_ids=true, to_apply=%region_15.16 | all-reduce | flops 1 | bytes 8 | tf_op jit(solution)/shard_map/psum | solution.py:39
  813.3 3.5 collective-permute-start.12
  818.7 3.8 collective-permute-done.13
  823.6 121.6 %all-reduce.17.cloned.1.call-done = f32[2,128,256]{2,1,0:T(8,128)} async-done(((f32[2,128,256]{2,1,0:T(8,128)}), f32[2,128,256]{2,1,0:T(8,128)}) %all-reduce.17.cloned.1.call-update) | async-done | bytes 262160 | tf_op jit(solution)/shard_map/psum | solution.py:33
  947.5 4.0 collective-permute-start.15
  952.0 1.5 collective-permute-done.15
  954.2 118.3 %psum.149 = f32[]{:T(128)} all-reduce(f32[]{:T(128)} %fusion), channel_id=1, replica_groups=mesh['samp'=8,'field'=64] {'field'}, use_global_device_ids=true, to_apply=%region_19.20 | all-reduce | flops 1 | bytes 8 | tf_op jit(solution)/shard_map/psum | solution.py:43
  1078.1 3.8 collective-permute-done.17
  1083.0 94.0 %all-reduce.19.cloned.1.call-done = f32[2,128,256]{2,1,0:T(8,128)} async-done(((f32[2,128,256]{2,1,0:T(8,128)}), f32[2,128,256]{2,1,0:T(8,128)}) %all-reduce.19.cloned.1.call-update) | async-done | bytes 262160 | tf_op jit(solution)/shard_map/psum | solution.py:33
  1179.3 4.0 collective-permute-start.19
  1183.7 1.5 collective-permute-done.19
  1185.3 4.1 collective-permute-start.20
  1191.3 3.8 collective-permute-done.21
  1196.2 79.0 %all-reduce.21.cloned.1.call-done = f32[2,128,256]{2,1,0:T(8,128)} async-done(((f32[2,128,256]{2,1,0:T(8,128)}), f32[2,128,256]{2,1,0:T(8,128)}) %all-reduce.21.cloned.1.call-update) | async-done | bytes 262160 | tf_op jit(solution)/shard_map/psum | solution.py:33
  1277.5 4.0 collective-permute-start.23
  1281.9 1.5 collective-permute-done.23
  1284.1 118.3 %all-reduce = (f32[]{:T(128)}, f32[]{:T(128)}) all-reduce(f32[]{:T(128)} %get-tuple-element.3, f32[]{:T(128)} %get-tuple-element.2), channel_id=1, replica_groups=mesh['samp'=8,'field'=64] {'field'}, use_global_device_ids=true, to_apply=%region_23.24 | all-reduce | flops 2 | bytes 16 | tf_op jit(solution)/shard_map/psum | solution.py:39
  1404.5 111.0 %psum.154 = f32[]{:T(128)} all-reduce(f32[]{:T(128)} %multiply_reduce_fusion.3), channel_id=1, replica_groups=mesh['samp'=8,'field'=64] {'field'}, use_global_device_ids=true, to_apply=%region_29.30 | all-reduce | flops 1 | bytes 8 | tf_op jit(solution)/shard_map/psum | solution.py:39
  1516.9 3.5 collective-permute-start.24
  1522.3 3.8 collective-permute-done.25
  1527.2 121.6 %all-reduce.23.cloned.1.call-done = f32[2,128,256]{2,1,0:T(8,128)} async-done(((f32[2,128,256]{2,1,0:T(8,128)}), f32[2,128,256]{2,1,0:T(8,128)}) %all-reduce.23.cloned.1.call-update) | async-done | bytes 262160 | tf_op jit(solution)/shard_map/psum | solution.py:33
  1651.2 4.0 collective-permute-start.27
  1655.6 1.5 collective-permute-done.27
  1657.8 118.3 %psum.156 = f32[]{:T(128)} all-reduce(f32[]{:T(128)} %multiply_reduce_fusion.2), channel_id=1, replica_groups=mesh['samp'=8,'field'=64] {'field'}, use_global_device_ids=true, to_apply=%region_33.34 | all-reduce | flops 1 | bytes 8 | tf_op jit(solution)/shard_map/psum | solution.py:43
  1778.1 110.9 %psum.157 = f32[]{:T(128)} all-reduce(f32[]{:T(128)} %get-tuple-element.10), channel_id=1, replica_groups=mesh['samp'=8,'field'=64] {'field'}, use_global_device_ids=true, to_apply=%region_35.36 | all-reduce | flops 1 | bytes 8 | tf_op jit(solution)/shard_map/psum | solution.py:39
  1890.4 3.5 collective-permute-start.28
  1895.9 3.8 collective-permute-done.29
  1900.7 121.7 %all-reduce.25.cloned.1.call-done = f32[2,128,256]{2,1,0:T(8,128)} async-done(((f32[2,128,256]{2,1,0:T(8,128)}), f32[2,128,256]{2,1,0:T(8,128)}) %all-reduce.25.cloned.1.call-update) | async-done | bytes 262160 | tf_op jit(solution)/shard_map/psum | solution.py:33
  2024.7 4.0 collective-permute-start.31
  2029.1 1.5 collective-permute-done.31
  2031.3 118.3 %psum.159 = f32[]{:T(128)} all-reduce(f32[]{:T(128)} %multiply_reduce_fusion), channel_id=1, replica_groups=mesh['samp'=8,'field'=64] {'field'}, use_global_device_ids=true, to_apply=%region_39.40 | all-reduce | flops 1 | bytes 8 | tf_op jit(solution)/shard_map/psum | solution.py:43
  (136 shorter events, 59.4 us)
Async XLA Ops:
  7.2 92.6 %all-reduce.11.cloned.1.call-start = ((), (), s32[]{:S(2)}) async-start(), calls=%async_computation | async-start | bytes 524288 | tf_op jit(solution)/shard_map/psum | solution.py:33
  8.3 6.3 collective-permute-start
  12.7 5.9 collective-permute-start.1
  20.3 87.7 %copy-start = (f32[2,128,256]{2,1,0:T(8,128)S(1)}, f32[2,128,256]{2,1,0:T(8,128)}, u32[]{:S(2)}) copy-start(f32[2,128,256]{2,1,0:T(8,128)} %param.6) | copy-start | bytes 786436
  20.3 177.6 %all-reduce.13.cloned.1.call-start = ((), (), s32[]{:S(2)}) async-start(), calls=%async_computation.1 | async-start | bytes 524288 | tf_op jit(solution)/shard_map/psum | solution.py:33
  99.8 8.3 copy-start.8
  100.8 5.7 collective-permute-start.2
  102.1 5.9 collective-permute-start.3
  108.2 6.0 collective-permute-start.4
  112.2 5.7 collective-permute-start.5
  118.9 452.7 %all-reduce.15.cloned.1.call-start = ((), (), s32[]{:S(2)}) async-start(), calls=%async_computation.2 | async-start | bytes 524288 | tf_op jit(solution)/shard_map/psum | solution.py:33
  198.0 8.3 copy-start.1
  199.0 5.7 collective-permute-start.6
  200.3 5.9 collective-permute-start.7
  439.7 5.5 collective-permute-start.8
  443.3 5.8 collective-permute-start.9
  450.0 495.2 %all-reduce.17.cloned.1.call-start = ((), (), s32[]{:S(2)}) async-start(), calls=%async_computation.3 | async-start | bytes 524288 | tf_op jit(solution)/shard_map/psum | solution.py:33
  571.7 8.3 copy-start.4
  572.7 5.7 collective-permute-start.10
  574.0 5.9 collective-permute-start.11
  813.3 5.5 collective-permute-start.12
  816.8 5.8 collective-permute-start.13
  823.5 353.4 %all-reduce.19.cloned.1.call-start = ((), (), s32[]{:S(2)}) async-start(), calls=%async_computation.4 | async-start | bytes 524288 | tf_op jit(solution)/shard_map/psum | solution.py:33
  945.2 8.3 copy-start.5
  946.2 5.7 collective-permute-start.14
  947.5 5.9 collective-permute-start.15
  1074.9 3.2 collective-permute-start.16
  1076.2 5.7 collective-permute-start.17
  1082.9 192.2 %all-reduce.21.cloned.1.call-start = ((), (), s32[]{:S(2)}) async-start(), calls=%async_computation.5 | async-start | bytes 524288 | tf_op jit(solution)/shard_map/psum | solution.py:33
  1177.0 8.3 copy-start.7
  1178.0 5.7 collective-permute-start.18
  1179.3 5.9 collective-permute-start.19
  1185.3 6.0 collective-permute-start.20
  1189.4 5.7 collective-permute-start.21
  1196.1 452.7 %all-reduce.23.cloned.1.call-start = ((), (), s32[]{:S(2)}) async-start(), calls=%async_computation.6 | async-start | bytes 524288 | tf_op jit(solution)/shard_map/psum | solution.py:33
  1275.1 8.3 copy-start.6
  1276.2 5.7 collective-permute-start.22
  1277.5 5.9 collective-permute-start.23
  1516.9 5.5 collective-permute-start.24
  1520.4 5.8 collective-permute-start.25
  1527.2 495.2 %all-reduce.25.cloned.1.call-start = ((), (), s32[]{:S(2)}) async-start(), calls=%async_computation.7 | async-start | bytes 524288 | tf_op jit(solution)/shard_map/psum | solution.py:33
  1648.8 8.3 copy-start.2
  1649.9 5.7 collective-permute-start.26
  1651.2 5.9 collective-permute-start.27
  1890.4 5.5 collective-permute-start.28
  1894.0 5.8 collective-permute-start.29
  2023.4 5.7 collective-permute-start.30
  2024.7 5.9 collective-permute-start.31
  (5 other events, 16.0 us)
Sparse Core Ops, SparseCore 0:
  20.4 79.3 all-reduce.10
  119.1 78.8 all-reduce.12
  450.1 121.4 all-reduce.14
  823.7 121.5 all-reduce.16
  1083.0 93.8 all-reduce.18
  1196.2 78.8 all-reduce.20
  1527.3 121.4 all-reduce.22
  1900.8 121.5 all-reduce.24
where the time goes:
time: 2190 us; the launch traced here: 2160 us
  blocking collectives  1150 us (53%)
  waiting for transfers between devices  869 us (40%)
  starting transfers between devices  81 us (4%)
  between operations  27.9 us (1%)
    psum x8, waiting for transfers between devices, average_back(): summed = lax.psum(term, 'samp')  818 us
    psum x6, blocking collectives, squares(): return lax.psum(jnp.sum(residual * residual), 'field')  680 us
    psum x4, blocking collectives, inner_product(): return lax.psum(jnp.sum(direction * image), 'field')  473 us
    ppermute x16, starting transfers between devices, padded_2(): lax.ppermute(tail, axis, [(i, (i + 1) % count) for i in range(ends)])  60 us
  transfers between devices with their start and end apart: 40, of which 40 were waited for; matrix products, arithmetic and copies ran while one was open for 0% of the time, Pallas kernels for 0%

commit v1 on v0

v1 whole, which is shorter than its diff:
```python
import functools

import jax
import jax.numpy as jnp
from jax import lax
from jax.experimental import pallas as pl
from jax.experimental.pallas import tpu as pltpu
from jax.sharding import Mesh, PartitionSpec as P

NEWTON = 2
ITERS = 3
PAIRS = 4
SAMPLES = 8
ROWS = 24
SHRINK = 2.0**-10
VMEM = 48 * 1024 * 1024


def shift_up(v, first):
    return jnp.where(first, 0.0, pltpu.roll(v, 1, 0))


def shift_down(v, last):
    return jnp.where(last, 0.0, pltpu.roll(v, v.shape[0] - 1, 0))


def edges(shape):
    row = lax.broadcasted_iota(jnp.int32, shape, 0)
    return row == 0, row == shape[0] - 1


def refine(v, taps, ends):
    even, odd = v
    return (
        taps[0] * shift_up(odd, ends[0]) + taps[1] * even + taps[2] * odd,
        taps[0] * even + taps[1] * odd + taps[2] * shift_down(even, ends[1]),
    )


def transpose_refine(u, taps, ends):
    even, odd = u
    return (
        taps[0] * odd + taps[1] * even + taps[2] * shift_up(odd, ends[0]),
        taps[0] * shift_down(even, ends[1]) + taps[1] * odd + taps[2] * even,
    )


def wide(column):
    return jnp.concatenate([column, column], axis=1)


def back(base, field, factors, weight, offset, taps, ends, scale):
    terms = []
    for p in range(2):
        w = base[p] if field is None else base[p] * field[p]
        total = None
        for k in range(SAMPLES):
            factor = factors[k, p]
            column = weight[p] * jnp.sum(factor * w, axis=1, keepdims=True)
            if offset is not None:
                column = column - offset[p]
            term = factor * wide(column)
            total = term if total is None else total + term
        terms.append(base[p] * total)
    return tuple(scale * t for t in transpose_refine(terms, taps, ends))


def dot(a, b):
    total = a[0] * b[0] + a[1] * b[1]
    total = jnp.sum(total[:, :128] + total[:, 128:], axis=0, keepdims=True)
    return jnp.sum(total, axis=1, keepdims=True)


def moments_row(basis):
    pairs = [(0, 0), (0, 1), (1, 1), (1, 2), (2, 2), (2, 3)]
    lane = lax.broadcasted_iota(jnp.int32, (1, 128), 1)
    row = jnp.zeros((1, 128), jnp.float32)
    for n, (i, j) in enumerate(pairs):
        row = jnp.where(lane == n, dot(basis[i], basis[j]), row)
    return row


def coefficients(row):
    lane = lax.broadcasted_iota(jnp.int32, (1, 128), 1)
    nu = [jnp.sum(jnp.where(lane == n, row, 0.0), axis=1, keepdims=True) for n in range(2 * ITERS)]
    zero, one = jnp.zeros((1, 1), jnp.float32), jnp.ones((1, 1), jnp.float32)

    def inner(a, b):
        total = zero
        for i, x in enumerate(a):
            for j, y in enumerate(b):
                if i + j < 2 * ITERS:
                    total = total + x * y * nu[i + j]
        return total

    def ratio(a, b):
        return jnp.where(b > 0.0, a / jnp.where(b > 0.0, b, 1.0), 0.0)

    residual = [one]
    direction = [one]
    step = [zero] * ITERS
    norm_now = nu[0]
    for it in range(ITERS):
        padded = direction + [zero]
        image = [padded[0]] + [padded[j] + (1.0 / SHRINK) * padded[j - 1] for j in range(1, len(padded))]
        alpha = ratio(norm_now, inner(direction, image))
        step = [s + alpha * direction[j] if j < len(direction) else s for j, s in enumerate(step)]
        residual = [r - alpha * i for r, i in zip(residual + [zero], image)]
        if it < ITERS - 1:
            norm_next = inner(residual, residual)
            beta = ratio(norm_next, norm_now)
            direction = [r + beta * d for r, d in zip(residual, direction + [zero])]
            norm_now = norm_next
    return step, residual


def combine(coefs, basis):
    out = []
    for p in range(2):
        total = coefs[0] * basis[0][p]
        for c, b in zip(coefs[1:], basis[1:]):
            total = total + c * b[p]
        out.append(total)
    return tuple(out)


def krylov(latent, factors, weight, offset, taps, ends):
    base = tuple(jnp.exp(t) for t in refine(latent, taps, ends))
    pulled = back(base, None, factors, weight, offset, taps, ends, 1.0 / SAMPLES)
    basis = [tuple(-m - t for m, t in zip(latent, pulled))]
    for _ in range(ITERS):
        basis.append(
            back(base, refine(basis[-1], taps, ends), factors, weight, None, taps, ends, SHRINK / SAMPLES)
        )
    return basis


def pack_kernel(member, mean, draws, mask, noise, data, out, block, *, count, copies, lines):
    first = member[0] * count
    for a in range(1 + PAIRS):
        for p in range(2):
            for h in range(2):
                lanes = slice(h * 128, h * 128 + 128)
                rows = mean[p, :, lanes] if a == 0 else draws[a - 1, p, :, lanes]
                block[pl.ds(a * 4 + p * 2 + h, count, stride=ROWS), :] = rows
    row = lax.broadcasted_iota(jnp.int32, (count, 128), 0)
    lane = lax.broadcasted_iota(jnp.int32, (count, 128), 1)
    mine = lane == row + first
    noisy = mask[...].astype(jnp.float32) * noise[...]
    for n, values in enumerate((noisy * (1.0 / 256.0), noisy * data[...])):
        for p in range(2):
            picked = jnp.sum(jnp.where(mine, values[p : p + 1, :], 0.0), axis=1, keepdims=True)
            block[pl.ds(20 + n * 2 + p, count, stride=ROWS), :] = jnp.broadcast_to(picked, (count, 128))
    chunk = lines * ROWS
    for fy in range(count // lines):
        for c in range(copies):
            out[pl.ds((fy * copies + c) * chunk, chunk), :] = block[pl.ds(fy * chunk, chunk), :]


def plane_rows(ref, a, p, n):
    return jnp.concatenate([ref[pl.ds(a * 4 + p * 2 + h, n, stride=ROWS), :] for h in range(2)], axis=1)


def columns(ref, n):
    weight = [ref[pl.ds(20 + p, n, stride=ROWS), :] for p in range(2)]
    offset = [ref[pl.ds(22 + p, n, stride=ROWS), :] for p in range(2)]
    return weight, offset


def first_kernel(packed, kernel, sums, factors, held, *, n):
    taps = [kernel[t : t + 1, :] for t in range(3)]
    ends = edges((n, 256))
    latent = tuple(plane_rows(packed, 0, p, n) for p in range(2))
    for k in range(PAIRS):
        spread = refine(tuple(plane_rows(packed, 1 + k, p, n) for p in range(2)), taps, ends)
        for p in range(2):
            factors[2 * k, p] = jnp.exp(spread[p])
            factors[2 * k + 1, p] = jnp.exp(-spread[p])
    weight, offset = columns(packed, n)
    basis = krylov(latent, factors, weight, offset, taps, ends)
    for p in range(2):
        held[0, p] = latent[p]
        for j in range(ITERS):
            held[1 + j, p] = basis[j][p]
    sums[...] = jnp.broadcast_to(moments_row(basis), sums.shape)


def second_kernel(place, sums, packed, kernel, factors, held, out, block, *, n, groups, lines):
    taps = [kernel[t : t + 1, :] for t in range(3)]
    ends = edges((n, 256))
    step, _ = coefficients(jnp.sum(sums[...], axis=0, keepdims=True))
    basis = [tuple(held[j, p] for p in range(2)) for j in range(1 + ITERS)]
    latent = combine([jnp.ones((1, 1), jnp.float32)] + step, basis)
    weight, offset = columns(packed, n)
    basis = krylov(latent, factors, weight, offset, taps, ends)
    for a, v in enumerate([latent] + basis):
        for p in range(2):
            for h in range(2):
                block[pl.ds(a * 4 + p * 2 + h, n, stride=ROWS), :] = v[p][:, h * 128 : h * 128 + 128]
    chunk = lines * ROWS
    for fy in range(groups):
        start = pl.multiple_of(fy * (n // groups) * ROWS + place[0] * chunk, 8)
        out[pl.ds(fy * chunk, chunk), :] = block[pl.ds(start, chunk), :]
    row = jnp.broadcast_to(moments_row(basis), (groups * lines, 128))
    for r in range(20, ROWS):
        out[pl.ds(r, groups * lines, stride=ROWS), :] = row


def last_kernel(gathered, mean_final, cg_residual, *, order, count):
    n = len(order) * count
    step, residual = coefficients(jnp.sum(gathered[pl.ds(20, n, stride=ROWS), :], axis=0, keepdims=True))
    for q, member in enumerate(order):
        for p in range(2):
            for h in range(2):
                v = [
                    gathered[pl.ds(q * count * ROWS + a * 4 + p * 2 + h, count, stride=ROWS), :]
                    for a in range(2 + ITERS)
                ]
                latent = v[0]
                for c, b in zip(step, v[1:]):
                    latent = latent + c * b
                rest = residual[0] * v[1]
                for c, b in zip(residual[1:], v[2:]):
                    rest = rest + c * b
                where = (p, slice(member * count, member * count + count), slice(h * 128, h * 128 + 128))
                mean_final[where] = latent
                cg_residual[where] = rest


def local(mean_start, sample_draws, kernel, sight_mask, noise_weight, data):
    nx, nc, nfy, nzq, nzl = (lax.axis_size(a) for a in ("x", "core", "fy", "zq", "zl"))
    members = nx * nc
    fields = nfy * nzq * nzl
    count = mean_start.shape[1] // members
    depth = mean_start.shape[2]
    f32 = functools.partial(jax.ShapeDtypeStruct, dtype=jnp.float32)
    params = pltpu.CompilerParams(vmem_limit_bytes=VMEM)
    whole = pl.BlockSpec(memory_space=pltpu.VMEM)
    member = (lax.axis_index("x") * nc + lax.axis_index("core")).astype(jnp.int32).reshape(1)
    place = lax.axis_index("zq").astype(jnp.int32).reshape(1)

    packed = pl.pallas_call(
        functools.partial(pack_kernel, count=count, copies=nzq, lines=nzl),
        out_shape=f32((fields * ROWS, 128)),
        grid_spec=pltpu.PrefetchScalarGridSpec(
            num_scalar_prefetch=1,
            grid=(1,),
            in_specs=[
                pl.BlockSpec((2, count, depth), lambda i, s: (0, s[0], 0)),
                pl.BlockSpec((PAIRS, 2, count, depth), lambda i, s: (0, 0, s[0], 0)),
                pl.BlockSpec(sight_mask.shape, lambda i, s: (0, 0)),
                pl.BlockSpec(noise_weight.shape, lambda i, s: (0, 0)),
                pl.BlockSpec(data.shape, lambda i, s: (0, 0)),
            ],
            out_specs=pl.BlockSpec((fields * ROWS, 128), lambda i, s: (0, 0)),
            scratch_shapes=[pltpu.VMEM((count * ROWS, 128), jnp.float32)],
        ),
        compiler_params=params,
        name="pack",
    )(member, mean_start, sample_draws, sight_mask, noise_weight, data)

    packed = lax.all_to_all(packed.reshape(fields, ROWS, 128), ("fy", "zq", "zl"), 0, 0, tiled=True)
    packed = packed.reshape(fields * ROWS, 128)

    cube = members * nfy * nzl
    sums, factors, held = pl.pallas_call(
        functools.partial(first_kernel, n=fields),
        out_shape=[
            f32((cube, 128)),
            f32((SAMPLES, 2, fields, depth)),
            f32((1 + ITERS, 2, fields, depth)),
        ],
        in_specs=[whole, whole],
        out_specs=[whole, whole, whole],
        compiler_params=params,
        name="first",
    )(packed, kernel)

    sums = lax.all_to_all(sums.reshape(cube, 1, 128), ("x", "core", "fy", "zl"), 0, 0, tiled=True)
    sums = sums.reshape(cube, 128)

    lines = nfy * nzl
    found = pl.pallas_call(
        functools.partial(second_kernel, n=fields, groups=nfy, lines=nzl),
        out_shape=f32((lines * ROWS, 128)),
        in_specs=[pl.BlockSpec(memory_space=pltpu.SMEM)] + [whole] * 5,
        out_specs=whole,
        scratch_shapes=[pltpu.VMEM((fields * ROWS, 128), jnp.float32)],
        compiler_params=params,
        name="second",
    )(place, sums, packed, kernel, factors, held)

    found = lax.all_to_all(found.reshape(lines, ROWS, 128), ("fy", "zl"), 0, 0, tiled=True)
    found = lax.all_gather(found.reshape(lines * ROWS, 128), "x")
    found = lax.all_gather(found.reshape(nx * lines * ROWS, 128), "core")
    found = found.reshape(members * lines * ROWS, 128)

    order = tuple(x * nc + c for c in range(nc) for x in range(nx))
    return pl.pallas_call(
        functools.partial(last_kernel, order=order, count=count),
        out_shape=[f32(mean_start.shape), f32(mean_start.shape)],
        in_specs=[whole],
        out_specs=[whole, whole],
        compiler_params=params,
        name="last",
    )(found)


def solution(mesh):
    split = Mesh(mesh.devices.reshape(4, 2, 4, 4, 4), ("x", "core", "fy", "zq", "zl"))
    field = ("fy", "zq", "zl")
    placed = (
        P(field, None, None),
        P(None, field, None, None),
        P(),
        P(field, None),
        P(field, None),
        P(field, None),
    )
    return jax.shard_map(
        local,
        mesh=split,
        in_specs=placed,
        out_specs=(P(field, None, None), P(field, None, None)),
        check_vma=False,
    )
```

time: 2190 us -> 145 us (0.07); the launches traced: 2160 us -> 144 us
  blocking collectives: 1150 us -> 81.8 us
  waiting for transfers between devices: 869 us -> 24.8 us
  starting transfers between devices: 81 us -> 13.2 us
    psum x10 -> x0, blocking collectives: 1150 us -> none  [the longest x6 680 us: squares(): return lax.psum(jnp.sum(residual * residual), 'field')]
    psum x8 -> x0, waiting for transfers between devices: 818 us -> none  [average_back(): summed = lax.psum(term, 'samp')]
    ppermute x32 -> x0, starting transfers between devices: 80.6 us -> none  [the longest x16 60 us: padded_2(): lax.ppermute(tail, axis, [(i, (i + 1) % count) for i in range(ends)])]
    all_to_all x0 -> x2, blocking collectives: none -> 69 us  [the longest x1 58.9 us: local(): lax.all_to_all(packed.reshape(fields, ROWS, 128), ('fy', 'zq', 'zl'), 0,...]
    ppermute x32 -> x0, waiting for transfers between devices: 51 us -> none  [the longest x16 33.9 us: padded_2(): lax.ppermute(head, axis, [((i + 1) % count, i) for i in range(ends)])]
  transfers between devices with their start and end apart: 40 -> 2, of which waited for: 40 -> 2; matrix products, arithmetic and copies ran while one was open for 0% -> 0% of each run, Pallas kernels for 0% -> 0%
where the time goes in v1:
time: 145 us; the launch traced here: 144 us
  blocking collectives  81.8 us (56%)
  waiting for transfers between devices  24.8 us (17%)
  between operations  14.1 us (10%)
  starting transfers between devices  13.2 us (9%)
  local copies, waits for them, and re-layouts  5.61 us (4%)
  Pallas kernels  4.74 us (3%)
    all_to_all x1, blocking collectives, local(): lax.all_to_all(packed.reshape(fields, ROWS, 128), ('fy', 'zq', 'zl'), 0,...  58.9 us
    all_gather x1, waiting for transfers between devices, local(): found = lax.all_gather(found.reshape(nx * lines * ROWS, 128), 'core')  15.3 us
    all_to_all x1, starting transfers between devices, local(): lax.all_to_all(sums.reshape(cube, 1, 128), ('x', 'core', 'fy', 'zl'), 0,...  13.2 us
    all_gather x1, blocking collectives, local(): found = lax.all_gather(found.reshape(lines * ROWS, 128), 'x')  12.8 us
    all_to_all x1, blocking collectives, local(): lax.all_to_all(found.reshape(lines, ROWS, 128), ('fy', 'zl'), 0, 0, tiled...  10.1 us
    all_to_all x1, waiting for transfers between devices, local(): lax.all_to_all(sums.reshape(cube, 1, 128), ('x', 'core', 'fy', 'zl'), 0,...  9.5 us
    unnamed x14, local copies, waits for them, and re-layouts  5.61 us
  transfers between devices with their start and end apart: 2, of which 2 were waited for; matrix products, arithmetic and copies ran while one was open for 0% of the time, Pallas kernels for 0%

profile of v1, /device:TPU:1, one launch (start us, length us, event | category | flops | bytes accessed | tf_op | source)
XLA Modules:
  0.0 144.3 jit_solution(8245818742735523567)
XLA Ops:
  7.2 0.0 copy-start.1
  7.2 1.2 copy-done.1
  8.4 0.0 copy-start.2
  8.4 0.9 copy-done.2
  9.3 0.0 copy-start.4
  9.4 0.7 copy-done.4
  10.0 0.0 copy-start.5
  10.0 0.7 copy-done.5
  10.7 0.0 copy-start.6
  10.7 0.7 copy-done.6
  11.4 0.0 copy-start.3
  11.4 0.1 pack.1
  11.5 58.9 %all_to_all.15 = f32[64,24,128]{2,1,0:T(8,128)S(1)} all-to-all(f32[64,24,128]{2,1,0:T(8,128)S(1)} %bitcast.14), channel_id=1, replica_groups=mesh['x'=4,'core'=2,'fy'=4,'zq'=4,'zl'=4] {'fy','zq','zl'}, dimensions={0} | all-to-all | bytes 1572864 | tf_op jit(solution)/shard_map/all_to_all | solution.py:262
  70.4 0.0 copy-done.3
  70.4 2.0 %first.1 = (f32[128,128]{1,0:T(8,128)}, f32[8,2,64,256]{3,2,1,0:T(8,128)S(1)}, f32[4,2,64,256]{3,2,1,0:T(8,128)S(1)}) custom-call(f32[1536,128]{1,0:T(8,128)S(1)} %bitcast.12, f32[3,256]{1,0:T(4,128)S(1)} %copy-done.3), custom_call_target="tpu_custom_call" | custom-call | tf_op jit(solution)/shard_map/first/pallas_call | solution.py:266
  72.4 13.2 %all-to-all-start.1 = ((f32[128,1,128]{2,1,0:T(1,128)}), f32[128,1,128]{2,1,0:T(1,128)S(1)}, u32[]{:S(2)}, u32[]{:S(2)}) async-start(f32[128,1,128]{2,1,0:T(1,128)} %bitcast.5), calls=%async_computation.1 | async-start | bytes 131072 | tf_op jit(solution)/shard_map/all_to_all | solution.py:279
  85.6 0.0 all-gather.2.cloned.1.call-start
  85.7 9.5 %all-to-all-done.1 = f32[128,1,128]{2,1,0:T(1,128)S(1)} async-done(((f32[128,1,128]{2,1,0:T(1,128)}), f32[128,1,128]{2,1,0:T(1,128)S(1)}, u32[]{:S(2)}, u32[]{:S(2)}) %all-to-all-start.1) | async-done | bytes 65568 | tf_op jit(solution)/shard_map/all_to_all | solution.py:279
  95.2 1.4 second.1
  96.6 10.1 %all_to_all.16 = f32[16,24,128]{2,1,0:T(8,128)S(1)} all-to-all(f32[16,24,128]{2,1,0:T(8,128)S(1)} %bitcast.16), channel_id=1, replica_groups=mesh['x'=4,'core'=2,'fy'=4,'zq'=4,'zl'=4] {'fy','zl'}, dimensions={0} | all-to-all | bytes 393216 | tf_op jit(solution)/shard_map/all_to_all | solution.py:293
  106.7 12.8 %all_gather.6 = f32[4,384,128]{2,1,0:T(8,128)} all-gather(f32[1,384,128]{2,1,0:T(8,128)S(1)} %bitcast.19), channel_id=1, replica_groups=mesh['x'=4,'core'=2,'fy'=4,'zq'=4,'zl'=4] {'x'}, dimensions={0}, use_global_device_ids=true | all-gather | bytes 983040 | tf_op jit(solution)/shard_map/all_gather | solution.py:294
  119.5 0.0 all-gather.2.cloned.1.call-update
  119.5 15.3 %all-gather.2.cloned.1.call-done = f32[2,1536,128]{2,1,0:T(8,128)} async-done(((f32[1,1536,128]{2,1,0:T(8,128)}), f32[2,1536,128]{2,1,0:T(8,128)}) %all-gather.2.cloned.1.call-update) | async-done | bytes 1572880 | tf_op jit(solution)/shard_map/all_gather | solution.py:295
  134.8 0.0 copy-start
  134.8 1.4 copy-done
  136.3 1.2 last.1
Async XLA Ops:
  7.2 1.2 copy-start.1
  8.4 0.9 copy-start.2
  9.3 0.7 copy-start.4
  10.0 0.7 copy-start.5
  10.7 0.7 copy-start.6
  11.4 59.0 %copy-start.3 = (f32[3,256]{1,0:T(4,128)S(1)}, f32[3,256]{1,0:T(4,128)}, u32[]{:S(2)}) copy-start(f32[3,256]{1,0:T(4,128)} %kernel.3) | copy-start | bytes 9220
  72.4 22.7 %all-to-all-start.1 = ((f32[128,1,128]{2,1,0:T(1,128)}), f32[128,1,128]{2,1,0:T(1,128)S(1)}, u32[]{:S(2)}, u32[]{:S(2)}) async-start(f32[128,1,128]{2,1,0:T(1,128)} %bitcast.5), calls=%async_computation.1 | async-start | bytes 131072 | tf_op jit(solution)/shard_map/all_to_all | solution.py:279
  85.6 49.2 %all-gather.2.cloned.1.call-start = ((), (), s32[]{:S(2)}) async-start(), calls=%async_computation.3 | async-start | bytes 2359296 | tf_op jit(solution)/shard_map/all_gather | solution.py:295
  134.8 1.4 copy-start
Sparse Core Ops, SparseCore 0:
  119.6 15.1 all-gather.1

commit v2 on v1

--- a/solution.py
+++ b/solution.py
@@ -14,6 +14,7 @@
 ROWS = 24
 SHRINK = 2.0**-10
 VMEM = 48 * 1024 * 1024
+FULL = 60 * 1024 * 1024
 
 
 def shift_up(v, first):
@@ -135,8 +136,28 @@
     return basis
 
 
-def pack_kernel(member, mean, draws, mask, noise, data, out, block, *, count, copies, lines):
-    first = member[0] * count
+def pack_kernel(
+    member, mean_all, draws_all, mask_all, noise_all, data_all, out,
+    mean, draws, mask, noise, data, block, sems, *, count, copies, lines,
+):
+    first = pl.multiple_of(member[0] * count, count)
+    mine = pl.ds(first, count)
+    loads = [
+        pltpu.make_async_copy(source, target, sems.at[n])
+        for n, (source, target) in enumerate(
+            [
+                (mean_all.at[:, mine, :], mean),
+                (draws_all.at[:, :, mine, :], draws),
+                (mask_all, mask),
+                (noise_all, noise),
+                (data_all, data),
+            ]
+        )
+    ]
+    for load in loads:
+        load.start()
+    for load in loads:
+        load.wait()
     for a in range(1 + PAIRS):
         for p in range(2):
             for h in range(2):
@@ -145,11 +166,11 @@
                 block[pl.ds(a * 4 + p * 2 + h, count, stride=ROWS), :] = rows
     row = lax.broadcasted_iota(jnp.int32, (count, 128), 0)
     lane = lax.broadcasted_iota(jnp.int32, (count, 128), 1)
-    mine = lane == row + first
+    chosen = lane == row + first
     noisy = mask[...].astype(jnp.float32) * noise[...]
     for n, values in enumerate((noisy * (1.0 / 256.0), noisy * data[...])):
         for p in range(2):
-            picked = jnp.sum(jnp.where(mine, values[p : p + 1, :], 0.0), axis=1, keepdims=True)
+            picked = jnp.sum(jnp.where(chosen, values[p : p + 1, :], 0.0), axis=1, keepdims=True)
             block[pl.ds(20 + n * 2 + p, count, stride=ROWS), :] = jnp.broadcast_to(picked, (count, 128))
     chunk = lines * ROWS
     for fy in range(count // lines):
@@ -206,25 +227,27 @@
         out[pl.ds(r, groups * lines, stride=ROWS), :] = row
 
 
-def last_kernel(gathered, mean_final, cg_residual, *, order, count):
-    n = len(order) * count
-    step, residual = coefficients(jnp.sum(gathered[pl.ds(20, n, stride=ROWS), :], axis=0, keepdims=True))
-    for q, member in enumerate(order):
-        for p in range(2):
-            for h in range(2):
-                v = [
-                    gathered[pl.ds(q * count * ROWS + a * 4 + p * 2 + h, count, stride=ROWS), :]
-                    for a in range(2 + ITERS)
-                ]
-                latent = v[0]
-                for c, b in zip(step, v[1:]):
-                    latent = latent + c * b
-                rest = residual[0] * v[1]
-                for c, b in zip(residual[1:], v[2:]):
-                    rest = rest + c * b
-                where = (p, slice(member * count, member * count + count), slice(h * 128, h * 128 + 128))
-                mean_final[where] = latent
-                cg_residual[where] = rest
+def last_kernel(core, found, other, mean_final, cg_residual, *, chips, count):
+    n = chips * count
+    sums = found[pl.ds(20, n, stride=ROWS), :] + other[pl.ds(20, n, stride=ROWS), :]
+    step, residual = coefficients(jnp.sum(sums, axis=0, keepdims=True))
+    for ref, owner in ((found, core[0]), (other, 1 - core[0])):
+        for x in range(chips):
+            rows = pl.ds(pl.multiple_of((2 * x + owner) * count, count), count)
+            for p in range(2):
+                for h in range(2):
+                    v = [
+                        ref[pl.ds(x * count * ROWS + a * 4 + p * 2 + h, count, stride=ROWS), :]
+                        for a in range(2 + ITERS)
+                    ]
+                    latent = v[0]
+                    for c, b in zip(step, v[1:]):
+                        latent = latent + c * b
+                    rest = residual[0] * v[1]
+                    for c, b in zip(residual[1:], v[2:]):
+                        rest = rest + c * b
+                    mean_final[p, rows, h * 128 : h * 128 + 128] = latent
+                    cg_residual[p, rows, h * 128 : h * 128 + 128] = rest
 
 
 def local(mean_start, sample_draws, kernel, sight_mask, noise_weight, data):
@@ -242,20 +265,18 @@
     packed = pl.pallas_call(
         functools.partial(pack_kernel, count=count, copies=nzq, lines=nzl),
         out_shape=f32((fields * ROWS, 128)),
-        grid_spec=pltpu.PrefetchScalarGridSpec(
-            num_scalar_prefetch=1,
-            grid=(1,),
-            in_specs=[
-                pl.BlockSpec((2, count, depth), lambda i, s: (0, s[0], 0)),
-                pl.BlockSpec((PAIRS, 2, count, depth), lambda i, s: (0, 0, s[0], 0)),
-                pl.BlockSpec(sight_mask.shape, lambda i, s: (0, 0)),
-                pl.BlockSpec(noise_weight.shape, lambda i, s: (0, 0)),
-                pl.BlockSpec(data.shape, lambda i, s: (0, 0)),
-            ],
-            out_specs=pl.BlockSpec((fields * ROWS, 128), lambda i, s: (0, 0)),
-            scratch_shapes=[pltpu.VMEM((count * ROWS, 128), jnp.float32)],
-        ),
-        compiler_params=params,
+        in_specs=[pl.BlockSpec(memory_space=pltpu.SMEM)] + [pl.BlockSpec(memory_space=pltpu.HBM)] * 5,
+        out_specs=whole,
+        scratch_shapes=[
+            pltpu.VMEM((2, count, depth), jnp.float32),
+            pltpu.VMEM((PAIRS, 2, count, depth), jnp.float32),
+            pltpu.VMEM(sight_mask.shape, jnp.int32),
+            pltpu.VMEM(noise_weight.shape, jnp.float32),
+            pltpu.VMEM(data.shape, jnp.float32),
+            pltpu.VMEM((count * ROWS, 128), jnp.float32),
+            pltpu.SemaphoreType.DMA((5,)),
+        ],
+        compiler_params=pltpu.CompilerParams(vmem_limit_bytes=FULL),
         name="pack",
     )(member, mean_start, sample_draws, sight_mask, noise_weight, data)
 
@@ -292,18 +313,17 @@
 
     found = lax.all_to_all(found.reshape(lines, ROWS, 128), ("fy", "zl"), 0, 0, tiled=True)
     found = lax.all_gather(found.reshape(lines * ROWS, 128), "x")
-    found = lax.all_gather(found.reshape(nx * lines * ROWS, 128), "core")
-    found = found.reshape(members * lines * ROWS, 128)
-
-    order = tuple(x * nc + c for c in range(nc) for x in range(nx))
+    found = found.reshape(nx * lines * ROWS, 128)
+    other = lax.ppermute(found, "core", [(0, 1), (1, 0)])
+    core = lax.axis_index("core").astype(jnp.int32).reshape(1)
     return pl.pallas_call(
-        functools.partial(last_kernel, order=order, count=count),
+        functools.partial(last_kernel, chips=nx, count=count),
         out_shape=[f32(mean_start.shape), f32(mean_start.shape)],
-        in_specs=[whole],
+        in_specs=[pl.BlockSpec(memory_space=pltpu.SMEM), whole, whole],
         out_specs=[whole, whole],
         compiler_params=params,
         name="last",
-    )(found)
+    )(core, found, other)
 
 
 def solution(mesh):

time: 145 us -> 120 us (0.83)
  between operations: 14.1 us -> 0.68 us
  waiting for transfers between devices: 24.8 us -> 11.4 us
  starting transfers between devices: 13.2 us -> 19.5 us
  local copies, waits for them, and re-layouts: 5.61 us -> 0.01 us
  Pallas kernels: 4.74 us -> 6.6 us
    all_gather x1 -> x0, waiting for transfers between devices: 15.3 us -> none  [local(): found = lax.all_gather(found.reshape(nx * lines * ROWS, 128), 'core')]
    ppermute x0 -> x1, starting transfers between devices: none -> 6.34 us  [local(): other = lax.ppermute(found, 'core', [(0, 1), (1, 0)])]
    unnamed x14 -> x2, local copies, waits for them, and re-layouts: 5.61 us -> 0.01 us
    ppermute x0 -> x1, waiting for transfers between devices: none -> 1.89 us  [local(): other = lax.ppermute(found, 'core', [(0, 1), (1, 0)])]
    pallas_call x1, Pallas kernels: 0.11 us -> 1.97 us  [local(): pl.pallas_call(functools.partial(pack_kernel, count=count, copies=nzq, li...]
where the time goes in v2:
time: 120 us; the launch traced here: 119 us
  blocking collectives  81 us (68%)
  starting transfers between devices  19.5 us (16%)
  waiting for transfers between devices  11.4 us (10%)
  Pallas kernels  6.6 us (6%)
    all_to_all x1, blocking collectives, local(): lax.all_to_all(packed.reshape(fields, ROWS, 128), ('fy', 'zq', 'zl'), 0,...  59.1 us
    all_to_all x1, starting transfers between devices, local(): lax.all_to_all(sums.reshape(cube, 1, 128), ('x', 'core', 'fy', 'zl'), 0,...  13.2 us
    all_gather x1, blocking collectives, local(): found = lax.all_gather(found.reshape(lines * ROWS, 128), 'x')  11.8 us
    all_to_all x1, blocking collectives, local(): lax.all_to_all(found.reshape(lines, ROWS, 128), ('fy', 'zl'), 0, 0, tiled...  10.1 us
    all_to_all x1, waiting for transfers between devices, local(): lax.all_to_all(sums.reshape(cube, 1, 128), ('x', 'core', 'fy', 'zl'), 0,...  9.55 us
    ppermute x1, starting transfers between devices, local(): other = lax.ppermute(found, 'core', [(0, 1), (1, 0)])  6.34 us
  transfers between devices with their start and end apart: 2, of which 2 were waited for; matrix products, arithmetic and copies ran while one was open for 0% of the time, Pallas kernels for 0%

profile of v2, /device:TPU:1, one launch (start us, length us, event | category | flops | bytes accessed | tf_op | source)
XLA Modules:
  0.0 119.2 jit_solution(1511062016554170165)
XLA Ops:
  0.6 2.0 %pack.1 = f32[1536,128]{1,0:T(8,128)} custom-call(s32[1]{0:T(128)} %bitcast.2.member, f32[2,128,256]{2,1,0:T(8,128)} %mean_all.1, f32[4,2,128,256]{3,2,1,0:T(8,128)} %draws_all.1, s32[2,128]{1,0:T(2,128)} %mask_all.1, f32[2,128]{1,0:T(2,128)} %noise_all.1, f32[2,128]{1,0:T(2,128)} %data_all.1), custom_call_target="tpu_custom_call" | custom-call | tf_op jit(solution)/shard_map/pack/pallas_call | solution.py:265
  2.6 0.0 copy-start
  2.6 59.1 %all_to_all.15 = f32[64,24,128]{2,1,0:T(8,128)S(1)} all-to-all(f32[64,24,128]{2,1,0:T(8,128)} %bitcast.18), channel_id=1, replica_groups=mesh['x'=4,'core'=2,'fy'=4,'zq'=4,'zl'=4] {'fy','zq','zl'}, dimensions={0} | all-to-all | bytes 1572864 | tf_op jit(solution)/shard_map/all_to_all | solution.py:283
  61.7 0.0 copy-done
  61.7 2.0 %first.1 = (f32[128,128]{1,0:T(8,128)}, f32[8,2,64,256]{3,2,1,0:T(8,128)S(1)}, f32[4,2,64,256]{3,2,1,0:T(8,128)S(1)}) custom-call(f32[1536,128]{1,0:T(8,128)S(1)} %bitcast.12, f32[3,256]{1,0:T(4,128)S(1)} %copy-done), custom_call_target="tpu_custom_call" | custom-call | tf_op jit(solution)/shard_map/first/pallas_call | solution.py:287
  63.8 13.2 %all-to-all-start.1 = ((f32[128,1,128]{2,1,0:T(1,128)}), f32[128,1,128]{2,1,0:T(1,128)S(1)}, u32[]{:S(2)}, u32[]{:S(2)}) async-start(f32[128,1,128]{2,1,0:T(1,128)} %bitcast.6), calls=%async_computation.1 | async-start | bytes 131072 | tf_op jit(solution)/shard_map/all_to_all | solution.py:300
  77.0 9.5 %all-to-all-done.1 = f32[128,1,128]{2,1,0:T(1,128)S(1)} async-done(((f32[128,1,128]{2,1,0:T(1,128)}), f32[128,1,128]{2,1,0:T(1,128)S(1)}, u32[]{:S(2)}, u32[]{:S(2)}) %all-to-all-start.1) | async-done | bytes 65568 | tf_op jit(solution)/shard_map/all_to_all | solution.py:300
  86.5 1.4 %second.1 = f32[384,128]{1,0:T(8,128)S(1)} custom-call(s32[1]{0:T(128)} %bitcast.1.place, f32[128,128]{1,0:T(8,128)S(1)} %bitcast.17, f32[1536,128]{1,0:T(8,128)S(1)} %bitcast.13, f32[3,256]{1,0:T(4,128)S(1)} %copy-done, f32[8,2,64,256]{3,2,1,0:T(8,128)S(1)} %get-tuple-element.6.factors, f32[4,2,64,256]{3,2,1,0:T(8,128)S(1)} %get-tuple-element.7.held), custom_call_target="tpu_custom_call" | custom-call | tf_op jit(solution)/shard_map/second/pallas_call | solution.py:304
  87.9 10.1 %all_to_all.16 = f32[16,24,128]{2,1,0:T(8,128)S(1)} all-to-all(f32[16,24,128]{2,1,0:T(8,128)S(1)} %bitcast.16), channel_id=1, replica_groups=mesh['x'=4,'core'=2,'fy'=4,'zq'=4,'zl'=4] {'fy','zl'}, dimensions={0} | all-to-all | bytes 393216 | tf_op jit(solution)/shard_map/all_to_all | solution.py:314
  98.0 11.8 %all_gather.3 = f32[4,384,128]{2,1,0:T(8,128)S(1)} all-gather(f32[1,384,128]{2,1,0:T(8,128)S(1)} %bitcast.19), channel_id=1, replica_groups=mesh['x'=4,'core'=2,'fy'=4,'zq'=4,'zl'=4] {'x'}, dimensions={0}, use_global_device_ids=true | all-gather | bytes 983040 | tf_op jit(solution)/shard_map/all_gather | solution.py:315
  109.8 6.3 %collective-permute-start = (f32[1536,128]{1,0:T(8,128)S(1)}, f32[1536,128]{1,0:T(8,128)S(1)}, u32[]{:S(2)}, u32[]{:S(2)}) collective-permute-start(f32[1536,128]{1,0:T(8,128)S(1)} %bitcast.14), channel_id=1, source_target_pairs={{0,64},{64,0},{1,65},{65,1},{2,66},{66,2},{3,67},{67,3},{4,68},{68... | collective-permute-start | bytes 2359304 | tf_op jit(solution)/shard_map/ppermute | solution.py:317
  116.1 1.9 %collective-permute-done.other = f32[1536,128]{1,0:T(8,128)S(1)} collective-permute-done((f32[1536,128]{1,0:T(8,128)S(1)}, f32[1536,128]{1,0:T(8,128)S(1)}, u32[]{:S(2)}, u32[]{:S(2)}) %collective-permute-start) | collective-permute-done | bytes 786464 | tf_op jit(solution)/shard_map/ppermute | solution.py:317
  118.0 1.2 last.1
Async XLA Ops:
  2.6 59.1 %copy-start = (f32[3,256]{1,0:T(4,128)S(1)}, f32[3,256]{1,0:T(4,128)}, u32[]{:S(2)}) copy-start(f32[3,256]{1,0:T(4,128)} %kernel.3) | copy-start | bytes 9220
  63.8 22.7 %all-to-all-start.1 = ((f32[128,1,128]{2,1,0:T(1,128)}), f32[128,1,128]{2,1,0:T(1,128)S(1)}, u32[]{:S(2)}, u32[]{:S(2)}) async-start(f32[128,1,128]{2,1,0:T(1,128)} %bitcast.6), calls=%async_computation.1 | async-start | bytes 131072 | tf_op jit(solution)/shard_map/all_to_all | solution.py:300
  109.8 8.2 %collective-permute-start = (f32[1536,128]{1,0:T(8,128)S(1)}, f32[1536,128]{1,0:T(8,128)S(1)}, u32[]{:S(2)}, u32[]{:S(2)}) collective-permute-start(f32[1536,128]{1,0:T(8,128)S(1)} %bitcast.14), channel_id=1, source_target_pairs={{0,64},{64,0},{1,65},{65,1},{2,66},{66,2},{3,67},{67,3},{4,68},{68... | collective-permute-start | bytes 2359304 | tf_op jit(solution)/shard_map/ppermute | solution.py:317

commit v3 on v2

--- a/solution.py
+++ b/solution.py
@@ -138,7 +138,7 @@
 
 def pack_kernel(
     member, mean_all, draws_all, mask_all, noise_all, data_all, out,
-    mean, draws, mask, noise, data, block, sems, *, count, copies, lines,
+    mean, draws, mask, noise, data, sems, *, count,
 ):
     first = pl.multiple_of(member[0] * count, count)
     mine = pl.ds(first, count)
@@ -163,7 +163,7 @@
             for h in range(2):
                 lanes = slice(h * 128, h * 128 + 128)
                 rows = mean[p, :, lanes] if a == 0 else draws[a - 1, p, :, lanes]
-                block[pl.ds(a * 4 + p * 2 + h, count, stride=ROWS), :] = rows
+                out[pl.ds(a * 4 + p * 2 + h, count, stride=ROWS), :] = rows
     row = lax.broadcasted_iota(jnp.int32, (count, 128), 0)
     lane = lax.broadcasted_iota(jnp.int32, (count, 128), 1)
     chosen = lane == row + first
@@ -171,11 +171,7 @@
     for n, values in enumerate((noisy * (1.0 / 256.0), noisy * data[...])):
         for p in range(2):
             picked = jnp.sum(jnp.where(chosen, values[p : p + 1, :], 0.0), axis=1, keepdims=True)
-            block[pl.ds(20 + n * 2 + p, count, stride=ROWS), :] = jnp.broadcast_to(picked, (count, 128))
-    chunk = lines * ROWS
-    for fy in range(count // lines):
-        for c in range(copies):
-            out[pl.ds((fy * copies + c) * chunk, chunk), :] = block[pl.ds(fy * chunk, chunk), :]
+            out[pl.ds(20 + n * 2 + p, count, stride=ROWS), :] = jnp.broadcast_to(picked, (count, 128))
 
 
 def plane_rows(ref, a, p, n):
@@ -206,7 +202,7 @@
     sums[...] = jnp.broadcast_to(moments_row(basis), sums.shape)
 
 
-def second_kernel(place, sums, packed, kernel, factors, held, out, block, *, n, groups, lines):
+def second_kernel(place, sums, packed, kernel, factors, held, out, block, *, n, lines):
     taps = [kernel[t : t + 1, :] for t in range(3)]
     ends = edges((n, 256))
     step, _ = coefficients(jnp.sum(sums[...], axis=0, keepdims=True))
@@ -219,12 +215,10 @@
             for h in range(2):
                 block[pl.ds(a * 4 + p * 2 + h, n, stride=ROWS), :] = v[p][:, h * 128 : h * 128 + 128]
     chunk = lines * ROWS
-    for fy in range(groups):
-        start = pl.multiple_of(fy * (n // groups) * ROWS + place[0] * chunk, 8)
-        out[pl.ds(fy * chunk, chunk), :] = block[pl.ds(start, chunk), :]
-    row = jnp.broadcast_to(moments_row(basis), (groups * lines, 128))
+    out[...] = block[pl.ds(pl.multiple_of(place[0] * chunk, 8), chunk), :]
+    row = jnp.broadcast_to(moments_row(basis), (lines, 128))
     for r in range(20, ROWS):
-        out[pl.ds(r, groups * lines, stride=ROWS), :] = row
+        out[pl.ds(r, lines, stride=ROWS), :] = row
 
 
 def last_kernel(core, found, other, mean_final, cg_residual, *, chips, count):
@@ -250,22 +244,30 @@
                     cg_residual[p, rows, h * 128 : h * 128 + 128] = rest
 
 
+def spread(block, axis):
+    copies = lax.axis_size(axis)
+    block = jnp.broadcast_to(block[None], (copies,) + block.shape)
+    return lax.all_to_all(block, axis, 0, 0, tiled=True)
+
+
 def local(mean_start, sample_draws, kernel, sight_mask, noise_weight, data):
-    nx, nc, nfy, nzq, nzl = (lax.axis_size(a) for a in ("x", "core", "fy", "zq", "zl"))
+    nx, nc, nfy, nfz = (lax.axis_size(a) for a in ("x", "core", "fy", "fz"))
     members = nx * nc
-    fields = nfy * nzq * nzl
+    fields = nfy * nfz
     count = mean_start.shape[1] // members
     depth = mean_start.shape[2]
     f32 = functools.partial(jax.ShapeDtypeStruct, dtype=jnp.float32)
     params = pltpu.CompilerParams(vmem_limit_bytes=VMEM)
     whole = pl.BlockSpec(memory_space=pltpu.VMEM)
-    member = (lax.axis_index("x") * nc + lax.axis_index("core")).astype(jnp.int32).reshape(1)
-    place = lax.axis_index("zq").astype(jnp.int32).reshape(1)
+    scalar = pl.BlockSpec(memory_space=pltpu.SMEM)
+    core = lax.axis_index("core").astype(jnp.int32)
+    member = (lax.axis_index("x").astype(jnp.int32) * nc + core).reshape(1)
+    place = lax.axis_index("fy").astype(jnp.int32).reshape(1)
 
     packed = pl.pallas_call(
-        functools.partial(pack_kernel, count=count, copies=nzq, lines=nzl),
-        out_shape=f32((fields * ROWS, 128)),
-        in_specs=[pl.BlockSpec(memory_space=pltpu.SMEM)] + [pl.BlockSpec(memory_space=pltpu.HBM)] * 5,
+        functools.partial(pack_kernel, count=count),
+        out_shape=f32((nfz * ROWS, 128)),
+        in_specs=[scalar] + [pl.BlockSpec(memory_space=pltpu.HBM)] * 5,
         out_specs=whole,
         scratch_shapes=[
             pltpu.VMEM((2, count, depth), jnp.float32),
@@ -273,21 +275,20 @@
             pltpu.VMEM(sight_mask.shape, jnp.int32),
             pltpu.VMEM(noise_weight.shape, jnp.float32),
             pltpu.VMEM(data.shape, jnp.float32),
-            pltpu.VMEM((count * ROWS, 128), jnp.float32),
             pltpu.SemaphoreType.DMA((5,)),
         ],
         compiler_params=pltpu.CompilerParams(vmem_limit_bytes=FULL),
         name="pack",
     )(member, mean_start, sample_draws, sight_mask, noise_weight, data)
 
-    packed = lax.all_to_all(packed.reshape(fields, ROWS, 128), ("fy", "zq", "zl"), 0, 0, tiled=True)
-    packed = packed.reshape(fields * ROWS, 128)
-
-    cube = members * nfy * nzl
+    packed = lax.all_to_all(packed.reshape(nfz, ROWS, 128), "fz", 0, 0, tiled=True)
+    packed = spread(packed.reshape(nfz * ROWS, 128), "fy").reshape(fields * ROWS, 128)
+
+    sharers = members * nfz
     sums, factors, held = pl.pallas_call(
         functools.partial(first_kernel, n=fields),
         out_shape=[
-            f32((cube, 128)),
+            f32((sharers, 128)),
             f32((SAMPLES, 2, fields, depth)),
             f32((1 + ITERS, 2, fields, depth)),
         ],
@@ -297,38 +298,36 @@
         name="first",
     )(packed, kernel)
 
-    sums = lax.all_to_all(sums.reshape(cube, 1, 128), ("x", "core", "fy", "zl"), 0, 0, tiled=True)
-    sums = sums.reshape(cube, 128)
-
-    lines = nfy * nzl
+    sums = lax.all_to_all(sums.reshape(sharers, 1, 128), ("x", "core", "fz"), 0, 0, tiled=True)
+    sums = sums.reshape(sharers, 128)
+
     found = pl.pallas_call(
-        functools.partial(second_kernel, n=fields, groups=nfy, lines=nzl),
-        out_shape=f32((lines * ROWS, 128)),
-        in_specs=[pl.BlockSpec(memory_space=pltpu.SMEM)] + [whole] * 5,
+        functools.partial(second_kernel, n=fields, lines=nfz),
+        out_shape=f32((nfz * ROWS, 128)),
+        in_specs=[scalar] + [whole] * 5,
         out_specs=whole,
         scratch_shapes=[pltpu.VMEM((fields * ROWS, 128), jnp.float32)],
         compiler_params=params,
         name="second",
     )(place, sums, packed, kernel, factors, held)
 
-    found = lax.all_to_all(found.reshape(lines, ROWS, 128), ("fy", "zl"), 0, 0, tiled=True)
-    found = lax.all_gather(found.reshape(lines * ROWS, 128), "x")
-    found = found.reshape(nx * lines * ROWS, 128)
+    found = lax.all_to_all(found.reshape(nfz, ROWS, 128), "fz", 0, 0, tiled=True)
+    found = spread(found.reshape(nfz * ROWS, 128), "x").reshape(nx * nfz * ROWS, 128)
     other = lax.ppermute(found, "core", [(0, 1), (1, 0)])
-    core = lax.axis_index("core").astype(jnp.int32).reshape(1)
+
     return pl.pallas_call(
         functools.partial(last_kernel, chips=nx, count=count),
         out_shape=[f32(mean_start.shape), f32(mean_start.shape)],
-        in_specs=[pl.BlockSpec(memory_space=pltpu.SMEM), whole, whole],
+        in_specs=[scalar, whole, whole],
         out_specs=[whole, whole],
         compiler_params=params,
         name="last",
-    )(core, found, other)
+    )(core.reshape(1), found, other)
 
 
 def solution(mesh):
-    split = Mesh(mesh.devices.reshape(4, 2, 4, 4, 4), ("x", "core", "fy", "zq", "zl"))
-    field = ("fy", "zq", "zl")
+    split = Mesh(mesh.devices.reshape(4, 2, 4, 16), ("x", "core", "fy", "fz"))
+    field = ("fy", "fz")
     placed = (
         P(field, None, None),
         P(None, field, None, None),

time: 120 us -> 119 us (level)
  the two profiles are of different devices: /device:TPU:1 before, /device:TPU:33 now
where the time goes in v3:
time: 119 us; the launch traced here: 118 us
  blocking collectives  78.7 us (66%)
  waiting for transfers between devices  16.5 us (14%)
  starting transfers between devices  16 us (13%)
  Pallas kernels  6.37 us (5%)
    all_to_all x1, blocking collectives, local(): lax.all_to_all(packed.reshape(nfz, ROWS, 128), 'fz', 0, 0, tiled=True)  30.5 us
    all_to_all x2, blocking collectives, spread(): return lax.all_to_all(block, axis, 0, 0, tiled=True)  28.5 us
    all_to_all x1, blocking collectives, local(): lax.all_to_all(found.reshape(nfz, ROWS, 128), 'fz', 0, 0, tiled=True)  19.7 us
    all_to_all x1, waiting for transfers between devices, local(): lax.all_to_all(sums.reshape(sharers, 1, 128), ('x', 'core', 'fz'), 0, 0,...  14.6 us
    all_to_all x1, starting transfers between devices, local(): lax.all_to_all(sums.reshape(sharers, 1, 128), ('x', 'core', 'fz'), 0, 0,...  12.1 us
    ppermute x1, starting transfers between devices, local(): other = lax.ppermute(found, 'core', [(0, 1), (1, 0)])  3.87 us
  transfers between devices with their start and end apart: 2, of which 2 were waited for; matrix products, arithmetic and copies ran while one was open for 0% of the time, Pallas kernels for 0%

profile of v3, /device:TPU:33, one launch (start us, length us, event | category | flops | bytes accessed | tf_op | source)
XLA Modules:
  0.0 118.3 jit_solution(11956778808545042955)
XLA Ops:
  0.6 1.7 %pack.1 = f32[384,128]{1,0:T(8,128)} custom-call(s32[1]{0:T(128)} %bitcast.2.member, f32[2,128,256]{2,1,0:T(8,128)} %mean_all.1, f32[4,2,128,256]{3,2,1,0:T(8,128)} %draws_all.1, s32[2,128]{1,0:T(2,128)} %mask_all.1, f32[2,128]{1,0:T(2,128)} %noise_all.1, f32[2,128]{1,0:T(2,128)} %data_all.1), custom_call_target="tpu_custom_call" | custom-call | tf_op jit(solution)/shard_map/pack/pallas_call | solution.py:267
  2.4 30.5 %all_to_all.25 = f32[16,24,128]{2,1,0:T(8,128)S(1)} all-to-all(f32[16,24,128]{2,1,0:T(8,128)} %bitcast.19), channel_id=1, replica_groups=mesh['x'=4,'core'=2,'fy'=4,'fz'=16] {'fz'}, dimensions={0} | all-to-all | bytes 393216 | tf_op jit(solution)/shard_map/all_to_all | solution.py:284
  32.9 0.1 broadcast_in_dim.15
  33.0 0.0 copy-start
  33.0 14.6 %all_to_all.26 = f32[4,384,128]{2,1,0:T(8,128)S(1)} all-to-all(f32[4,384,128]{2,1,0:T(8,128)S(1)} %broadcast_in_dim.15), channel_id=1, replica_groups=mesh['x'=4,'core'=2,'fy'=4,'fz'=16] {'fy'}, dimensions={0} | all-to-all | bytes 1572864 | tf_op jit(solution)/shard_map/all_to_all | solution.py:250
  47.6 0.0 copy-done
  47.6 2.0 %first.1 = (f32[128,128]{1,0:T(8,128)}, f32[8,2,64,256]{3,2,1,0:T(8,128)S(1)}, f32[4,2,64,256]{3,2,1,0:T(8,128)S(1)}) custom-call(f32[1536,128]{1,0:T(8,128)S(1)} %bitcast.13, f32[3,256]{1,0:T(4,128)S(1)} %copy-done), custom_call_target="tpu_custom_call" | custom-call | tf_op jit(solution)/shard_map/first/pallas_call | solution.py:288
  49.6 12.1 %all-to-all-start.2 = ((f32[128,1,128]{2,1,0:T(1,128)}), f32[128,1,128]{2,1,0:T(1,128)S(1)}, u32[]{:S(2)}, u32[]{:S(2)}) async-start(f32[128,1,128]{2,1,0:T(1,128)} %bitcast.7), calls=%async_computation.2 | async-start | bytes 131072 | tf_op jit(solution)/shard_map/all_to_all | solution.py:301
  61.8 14.6 %all-to-all-done.2 = f32[128,1,128]{2,1,0:T(1,128)S(1)} async-done(((f32[128,1,128]{2,1,0:T(1,128)}), f32[128,1,128]{2,1,0:T(1,128)S(1)}, u32[]{:S(2)}, u32[]{:S(2)}) %all-to-all-start.2) | async-done | bytes 65568 | tf_op jit(solution)/shard_map/all_to_all | solution.py:301
  76.3 1.4 %second.1 = f32[384,128]{1,0:T(8,128)S(1)} custom-call(s32[1]{0:T(128)} %bitcast.1.place, f32[128,128]{1,0:T(8,128)S(1)} %bitcast.18, f32[1536,128]{1,0:T(8,128)S(1)} %bitcast.14, f32[3,256]{1,0:T(4,128)S(1)} %copy-done, f32[8,2,64,256]{3,2,1,0:T(8,128)S(1)} %get-tuple-element.6.factors, f32[4,2,64,256]{3,2,1,0:T(8,128)S(1)} %get-tuple-element.7.held), custom_call_target="tpu_custom_call" | custom-call | tf_op jit(solution)/shard_map/second/pallas_call | solution.py:304
  77.7 19.7 %all_to_all.27 = f32[16,24,128]{2,1,0:T(8,128)S(1)} all-to-all(f32[16,24,128]{2,1,0:T(8,128)S(1)} %bitcast.17), channel_id=1, replica_groups=mesh['x'=4,'core'=2,'fy'=4,'fz'=16] {'fz'}, dimensions={0} | all-to-all | bytes 393216 | tf_op jit(solution)/shard_map/all_to_all | solution.py:314
  97.4 0.1 broadcast_in_dim.17
  97.5 13.9 %all_to_all.28 = f32[4,384,128]{2,1,0:T(8,128)S(1)} all-to-all(f32[4,384,128]{2,1,0:T(8,128)S(1)} %broadcast_in_dim.17), channel_id=1, replica_groups=mesh['x'=4,'core'=2,'fy'=4,'fz'=16] {'x'}, dimensions={0} | all-to-all | bytes 1572864 | tf_op jit(solution)/shard_map/all_to_all | solution.py:250
  111.4 3.9 %collective-permute-start = (f32[1536,128]{1,0:T(8,128)S(1)}, f32[1536,128]{1,0:T(8,128)S(1)}, u32[]{:S(2)}, u32[]{:S(2)}) collective-permute-start(f32[1536,128]{1,0:T(8,128)S(1)} %bitcast.15), channel_id=1, source_target_pairs={{0,64},{64,0},{1,65},{65,1},{2,66},{66,2},{3,67},{67,3},{4,68},{68... | collective-permute-start | bytes 2359304 | tf_op jit(solution)/shard_map/ppermute | solution.py:316
  115.3 1.9 %collective-permute-done.other = f32[1536,128]{1,0:T(8,128)S(1)} collective-permute-done((f32[1536,128]{1,0:T(8,128)S(1)}, f32[1536,128]{1,0:T(8,128)S(1)}, u32[]{:S(2)}, u32[]{:S(2)}) %collective-permute-start) | collective-permute-done | bytes 786464 | tf_op jit(solution)/shard_map/ppermute | solution.py:316
  117.2 1.2 last.1
Async XLA Ops:
  33.0 14.6 %copy-start = (f32[3,256]{1,0:T(4,128)S(1)}, f32[3,256]{1,0:T(4,128)}, u32[]{:S(2)}) copy-start(f32[3,256]{1,0:T(4,128)} %kernel.3) | copy-start | bytes 9220
  49.6 26.7 %all-to-all-start.2 = ((f32[128,1,128]{2,1,0:T(1,128)}), f32[128,1,128]{2,1,0:T(1,128)S(1)}, u32[]{:S(2)}, u32[]{:S(2)}) async-start(f32[128,1,128]{2,1,0:T(1,128)} %bitcast.7), calls=%async_computation.2 | async-start | bytes 131072 | tf_op jit(solution)/shard_map/all_to_all | solution.py:301
  111.4 5.8 %collective-permute-start = (f32[1536,128]{1,0:T(8,128)S(1)}, f32[1536,128]{1,0:T(8,128)S(1)}, u32[]{:S(2)}, u32[]{:S(2)}) collective-permute-start(f32[1536,128]{1,0:T(8,128)S(1)} %bitcast.15), channel_id=1, source_target_pairs={{0,64},{64,0},{1,65},{65,1},{2,66},{66,2},{3,67},{67,3},{4,68},{68... | collective-permute-start | bytes 2359304 | tf_op jit(solution)/shard_map/ppermute | solution.py:316

commit v4 on v3

--- a/solution.py
+++ b/solution.py
@@ -11,6 +11,7 @@
 ITERS = 3
 PAIRS = 4
 SAMPLES = 8
+IN = 21
 ROWS = 24
 SHRINK = 2.0**-10
 VMEM = 48 * 1024 * 1024
@@ -137,10 +138,10 @@
 
 
 def pack_kernel(
-    member, mean_all, draws_all, mask_all, noise_all, data_all, out,
-    mean, draws, mask, noise, data, sems, *, count,
+    code, mean_all, draws_all, mask_all, noise_all, data_all, out,
+    mean, draws, mask, noise, data, sems, *, count, members,
 ):
-    first = pl.multiple_of(member[0] * count, count)
+    first = pl.multiple_of((code[0] % members) * count, count)
     mine = pl.ds(first, count)
     loads = [
         pltpu.make_async_copy(source, target, sems.at[n])
@@ -163,25 +164,27 @@
             for h in range(2):
                 lanes = slice(h * 128, h * 128 + 128)
                 rows = mean[p, :, lanes] if a == 0 else draws[a - 1, p, :, lanes]
-                out[pl.ds(a * 4 + p * 2 + h, count, stride=ROWS), :] = rows
+                out[pl.ds(a * 4 + p * 2 + h, count, stride=IN), :] = rows
     row = lax.broadcasted_iota(jnp.int32, (count, 128), 0)
     lane = lax.broadcasted_iota(jnp.int32, (count, 128), 1)
     chosen = lane == row + first
     noisy = mask[...].astype(jnp.float32) * noise[...]
+    extra = jnp.zeros((count, 128), jnp.float32)
     for n, values in enumerate((noisy * (1.0 / 256.0), noisy * data[...])):
         for p in range(2):
             picked = jnp.sum(jnp.where(chosen, values[p : p + 1, :], 0.0), axis=1, keepdims=True)
-            out[pl.ds(20 + n * 2 + p, count, stride=ROWS), :] = jnp.broadcast_to(picked, (count, 128))
+            extra = jnp.where(lane == n * 2 + p, picked, extra)
+    out[pl.ds(20, count, stride=IN), :] = extra
 
 
 def plane_rows(ref, a, p, n):
-    return jnp.concatenate([ref[pl.ds(a * 4 + p * 2 + h, n, stride=ROWS), :] for h in range(2)], axis=1)
+    return jnp.concatenate([ref[pl.ds(a * 4 + p * 2 + h, n, stride=IN), :] for h in range(2)], axis=1)
 
 
 def columns(ref, n):
-    weight = [ref[pl.ds(20 + p, n, stride=ROWS), :] for p in range(2)]
-    offset = [ref[pl.ds(22 + p, n, stride=ROWS), :] for p in range(2)]
-    return weight, offset
+    extra = ref[pl.ds(20, n, stride=IN), :]
+    spread = [jnp.broadcast_to(extra[:, c : c + 1], extra.shape) for c in range(4)]
+    return spread[:2], spread[2:]
 
 
 def first_kernel(packed, kernel, sums, factors, held, *, n):
@@ -199,10 +202,10 @@
         held[0, p] = latent[p]
         for j in range(ITERS):
             held[1 + j, p] = basis[j][p]
-    sums[...] = jnp.broadcast_to(moments_row(basis), sums.shape)
-
-
-def second_kernel(place, sums, packed, kernel, factors, held, out, block, *, n, lines):
+    sums[...] = moments_row(basis)
+
+
+def second_kernel(code, sums, packed, kernel, factors, held, out, block, *, n, groups, lines, members):
     taps = [kernel[t : t + 1, :] for t in range(3)]
     ends = edges((n, 256))
     step, _ = coefficients(jnp.sum(sums[...], axis=0, keepdims=True))
@@ -215,17 +218,20 @@
             for h in range(2):
                 block[pl.ds(a * 4 + p * 2 + h, n, stride=ROWS), :] = v[p][:, h * 128 : h * 128 + 128]
     chunk = lines * ROWS
-    out[...] = block[pl.ds(pl.multiple_of(place[0] * chunk, 8), chunk), :]
-    row = jnp.broadcast_to(moments_row(basis), (lines, 128))
+    for fy in range(groups):
+        start = pl.multiple_of(fy * (n // groups) * ROWS + (code[0] // members) * chunk, 8)
+        out[pl.ds(fy * chunk, chunk), :] = block[pl.ds(start, chunk), :]
+    row = jnp.broadcast_to(moments_row(basis), (groups * lines, 128))
     for r in range(20, ROWS):
-        out[pl.ds(r, lines, stride=ROWS), :] = row
-
-
-def last_kernel(core, found, other, mean_final, cg_residual, *, chips, count):
+        out[pl.ds(r, groups * lines, stride=ROWS), :] = row
+
+
+def last_kernel(code, found, other, mean_final, cg_residual, *, chips, count):
+    core = code[0] % 2
     n = chips * count
     sums = found[pl.ds(20, n, stride=ROWS), :] + other[pl.ds(20, n, stride=ROWS), :]
     step, residual = coefficients(jnp.sum(sums, axis=0, keepdims=True))
-    for ref, owner in ((found, core[0]), (other, 1 - core[0])):
+    for ref, owner in ((found, core), (other, 1 - core)):
         for x in range(chips):
             rows = pl.ds(pl.multiple_of((2 * x + owner) * count, count), count)
             for p in range(2):
@@ -251,22 +257,22 @@
 
 
 def local(mean_start, sample_draws, kernel, sight_mask, noise_weight, data):
-    nx, nc, nfy, nfz = (lax.axis_size(a) for a in ("x", "core", "fy", "fz"))
+    nx, nc, nfy, nzq, nzl = (lax.axis_size(a) for a in ("x", "core", "fy", "zq", "zl"))
     members = nx * nc
-    fields = nfy * nfz
+    fields = nfy * nzq * nzl
+    lines = nfy * nzl
     count = mean_start.shape[1] // members
     depth = mean_start.shape[2]
     f32 = functools.partial(jax.ShapeDtypeStruct, dtype=jnp.float32)
     params = pltpu.CompilerParams(vmem_limit_bytes=VMEM)
     whole = pl.BlockSpec(memory_space=pltpu.VMEM)
     scalar = pl.BlockSpec(memory_space=pltpu.SMEM)
-    core = lax.axis_index("core").astype(jnp.int32)
-    member = (lax.axis_index("x").astype(jnp.int32) * nc + core).reshape(1)
-    place = lax.axis_index("fy").astype(jnp.int32).reshape(1)
+    code = lax.axis_index("zq") * members + lax.axis_index("x") * nc + lax.axis_index("core")
+    code = code.astype(jnp.int32).reshape(1)
 
     packed = pl.pallas_call(
-        functools.partial(pack_kernel, count=count),
-        out_shape=f32((nfz * ROWS, 128)),
+        functools.partial(pack_kernel, count=count, members=members),
+        out_shape=f32((lines * IN, 128)),
         in_specs=[scalar] + [pl.BlockSpec(memory_space=pltpu.HBM)] * 5,
         out_specs=whole,
         scratch_shapes=[
@@ -279,16 +285,17 @@
         ],
         compiler_params=pltpu.CompilerParams(vmem_limit_bytes=FULL),
         name="pack",
-    )(member, mean_start, sample_draws, sight_mask, noise_weight, data)
-
-    packed = lax.all_to_all(packed.reshape(nfz, ROWS, 128), "fz", 0, 0, tiled=True)
-    packed = spread(packed.reshape(nfz * ROWS, 128), "fy").reshape(fields * ROWS, 128)
-
-    sharers = members * nfz
+    )(code, mean_start, sample_draws, sight_mask, noise_weight, data)
+
+    packed = jnp.broadcast_to(packed.reshape(nfy, 1, nzl * IN, 1, 128), (nfy, nzq, nzl * IN, 1, 128))
+    packed = lax.all_to_all(packed.reshape(fields * IN, 1, 128), ("fy", "zq", "zl"), 0, 0, tiled=True)
+    packed = packed.reshape(fields * IN, 128)
+
+    sharers = members * lines
     sums, factors, held = pl.pallas_call(
         functools.partial(first_kernel, n=fields),
         out_shape=[
-            f32((sharers, 128)),
+            f32((1, 128)),
             f32((SAMPLES, 2, fields, depth)),
             f32((1 + ITERS, 2, fields, depth)),
         ],
@@ -298,21 +305,22 @@
         name="first",
     )(packed, kernel)
 
-    sums = lax.all_to_all(sums.reshape(sharers, 1, 128), ("x", "core", "fz"), 0, 0, tiled=True)
+    sums = jnp.broadcast_to(sums[None], (sharers, 1, 128))
+    sums = lax.all_to_all(sums, ("fy", "zl", "x", "core"), 0, 0, tiled=True)
     sums = sums.reshape(sharers, 128)
 
     found = pl.pallas_call(
-        functools.partial(second_kernel, n=fields, lines=nfz),
-        out_shape=f32((nfz * ROWS, 128)),
+        functools.partial(second_kernel, n=fields, groups=nfy, lines=nzl, members=members),
+        out_shape=f32((lines * ROWS, 128)),
         in_specs=[scalar] + [whole] * 5,
         out_specs=whole,
         scratch_shapes=[pltpu.VMEM((fields * ROWS, 128), jnp.float32)],
         compiler_params=params,
         name="second",
-    )(place, sums, packed, kernel, factors, held)
-
-    found = lax.all_to_all(found.reshape(nfz, ROWS, 128), "fz", 0, 0, tiled=True)
-    found = spread(found.reshape(nfz * ROWS, 128), "x").reshape(nx * nfz * ROWS, 128)
+    )(code, sums, packed, kernel, factors, held)
+
+    found = lax.all_to_all(found.reshape(lines, ROWS, 128), ("fy", "zl"), 0, 0, tiled=True)
+    found = spread(found.reshape(lines * ROWS, 128), "x").reshape(nx * lines * ROWS, 128)
     other = lax.ppermute(found, "core", [(0, 1), (1, 0)])
 
     return pl.pallas_call(
@@ -322,12 +330,12 @@
         out_specs=[whole, whole],
         compiler_params=params,
         name="last",
-    )(core.reshape(1), found, other)
+    )(code, found, other)
 
 
 def solution(mesh):
-    split = Mesh(mesh.devices.reshape(4, 2, 4, 16), ("x", "core", "fy", "fz"))
-    field = ("fy", "fz")
+    split = Mesh(mesh.devices.reshape(4, 2, 4, 4, 4), ("x", "core", "fy", "zq", "zl"))
+    field = ("fy", "zq", "zl")
     placed = (
         P(field, None, None),
         P(None, field, None, None),

time: 119 us -> 115 us (0.966)
  the two profiles are of different devices: /device:TPU:33 before, /device:TPU:1 now
where the time goes in v4:
time: 115 us
  blocking collectives  99.2 us (86%)
  Pallas kernels  5.9 us (5%)
  starting transfers between devices  5.86 us (5%)
  waiting for transfers between devices  1.89 us (2%)
    all_to_all x1, blocking collectives, local(): lax.all_to_all(packed.reshape(fields * IN, 1, 128), ('fy', 'zq', 'zl'), 0...  54.8 us
    all_to_all x1, blocking collectives, local(): sums = lax.all_to_all(sums, ('fy', 'zl', 'x', 'core'), 0, 0, tiled=True)  22.6 us
    all_to_all x1, blocking collectives, spread(): return lax.all_to_all(block, axis, 0, 0, tiled=True)  11.7 us
    all_to_all x1, blocking collectives, local(): lax.all_to_all(found.reshape(lines, ROWS, 128), ('fy', 'zl'), 0, 0, tiled...  10.1 us
    ppermute x1, starting transfers between devices, local(): other = lax.ppermute(found, 'core', [(0, 1), (1, 0)])  5.86 us
  transfers between devices with their start and end apart: 1, of which 1 were waited for; matrix products, arithmetic and copies ran while one was open for 0% of the time, Pallas kernels for 0%

profile of v4, /device:TPU:1, one launch (start us, length us, event | category | flops | bytes accessed | tf_op | source)
XLA Modules:
  0.0 114.7 jit_solution(6332889985785618330)
XLA Ops:
  0.6 1.7 %pack.1 = f32[336,128]{1,0:T(8,128)} custom-call(s32[1]{0:T(128)} %bitcast.code, f32[2,128,256]{2,1,0:T(8,128)} %mean_all.1, f32[4,2,128,256]{3,2,1,0:T(8,128)} %draws_all.1, s32[2,128]{1,0:T(2,128)} %mask_all.1, f32[2,128]{1,0:T(2,128)} %noise_all.1, f32[2,128]{1,0:T(2,128)} %data_all.1), custom_call_target="tpu_custom_call" | custom-call | tf_op jit(solution)/shard_map/pack/pallas_call | solution.py:273
  2.4 0.9 broadcast_in_dim.24
  3.4 0.0 copy-start
  3.4 54.8 %all_to_all.20 = f32[1344,1,128]{2,1,0:T(1,128)S(1)} all-to-all(f32[1344,1,128]{2,1,0:T(1,128)S(1)} %bitcast.15), channel_id=1, replica_groups=mesh['x'=4,'core'=2,'fy'=4,'zq'=4,'zl'=4] {'fy','zq','zl'}, dimensions={0} | all-to-all | bytes 1376256 | tf_op jit(solution)/shard_map/all_to_all | solution.py:291
  58.3 0.0 copy-done
  58.3 1.5 %first.1 = (f32[1,128]{1,0:T(1,128)S(1)}, f32[8,2,64,256]{3,2,1,0:T(8,128)S(1)}, f32[4,2,64,256]{3,2,1,0:T(8,128)S(1)}) custom-call(f32[1344,128]{1,0:T(8,128)S(1)} %bitcast.8, f32[3,256]{1,0:T(4,128)S(1)} %copy-done), custom_call_target="tpu_custom_call" | custom-call | tf_op jit(solution)/shard_map/first/pallas_call | solution.py:295
  59.8 22.6 %all_to_all.21 = f32[128,1,128]{2,1,0:T(1,128)S(1)} all-to-all(f32[128,1,128]{2,1,0:T(1,128)S(1)} %broadcast_in_dim.28), channel_id=1, replica_groups=mesh['x'=4,'core'=2,'fy'=4,'zq'=4,'zl'=4] {'fy','zl','x','core'}, dimensions={0} | all-to-all | bytes 131072 | tf_op jit(solution)/shard_map/all_to_all | solution.py:309
  82.4 1.5 %second.1 = f32[384,128]{1,0:T(8,128)S(1)} custom-call(s32[1]{0:T(128)} %bitcast.code, f32[128,128]{1,0:T(8,128)S(1)} %bitcast.13, f32[1344,128]{1,0:T(8,128)S(1)} %bitcast.9, f32[3,256]{1,0:T(4,128)S(1)} %copy-done, f32[8,2,64,256]{3,2,1,0:T(8,128)S(1)} %get-tuple-element.6.factors, f32[4,2,64,256]{3,2,1,0:T(8,128)S(1)} %get-tuple-element.7.held), custom_call_target="tpu_custom_call" | custom-call | tf_op jit(solution)/shard_map/second/pallas_call | solution.py:312
  83.9 10.1 %all_to_all.22 = f32[16,24,128]{2,1,0:T(8,128)S(1)} all-to-all(f32[16,24,128]{2,1,0:T(8,128)S(1)} %bitcast.12), channel_id=1, replica_groups=mesh['x'=4,'core'=2,'fy'=4,'zq'=4,'zl'=4] {'fy','zl'}, dimensions={0} | all-to-all | bytes 393216 | tf_op jit(solution)/shard_map/all_to_all | solution.py:322
  94.0 0.1 broadcast_in_dim.30
  94.1 11.7 %all_to_all.23 = f32[4,384,128]{2,1,0:T(8,128)S(1)} all-to-all(f32[4,384,128]{2,1,0:T(8,128)S(1)} %broadcast_in_dim.30), channel_id=1, replica_groups=mesh['x'=4,'core'=2,'fy'=4,'zq'=4,'zl'=4] {'x'}, dimensions={0} | all-to-all | bytes 1572864 | tf_op jit(solution)/shard_map/all_to_all | solution.py:256
  105.7 5.9 %collective-permute-start = (f32[1536,128]{1,0:T(8,128)S(1)}, f32[1536,128]{1,0:T(8,128)S(1)}, u32[]{:S(2)}, u32[]{:S(2)}) collective-permute-start(f32[1536,128]{1,0:T(8,128)S(1)} %bitcast.10), channel_id=1, source_target_pairs={{0,64},{64,0},{1,65},{65,1},{2,66},{66,2},{3,67},{67,3},{4,68},{68... | collective-permute-start | bytes 2359304 | tf_op jit(solution)/shard_map/ppermute | solution.py:324
  111.6 1.9 %collective-permute-done.other = f32[1536,128]{1,0:T(8,128)S(1)} collective-permute-done((f32[1536,128]{1,0:T(8,128)S(1)}, f32[1536,128]{1,0:T(8,128)S(1)}, u32[]{:S(2)}, u32[]{:S(2)}) %collective-permute-start) | collective-permute-done | bytes 786464 | tf_op jit(solution)/shard_map/ppermute | solution.py:324
  113.5 1.2 %last.1 = (f32[2,128,256]{2,1,0:T(8,128)}, f32[2,128,256]{2,1,0:T(8,128)}) custom-call(s32[1]{0:T(128)} %bitcast.code, f32[1536,128]{1,0:T(8,128)S(1)} %bitcast.11, f32[1536,128]{1,0:T(8,128)S(1)} %collective-permute-done.other), custom_call_target="tpu_custom_call" | custom-call | tf_op jit(solution)/shard_map/last/pallas_call | solution.py:326
  (3 shorter events, 0.1 us)
Async XLA Ops:
  3.4 54.9 %copy-start = (f32[3,256]{1,0:T(4,128)S(1)}, f32[3,256]{1,0:T(4,128)}, u32[]{:S(2)}) copy-start(f32[3,256]{1,0:T(4,128)} %kernel.3) | copy-start | bytes 9220
  105.7 7.8 %collective-permute-start = (f32[1536,128]{1,0:T(8,128)S(1)}, f32[1536,128]{1,0:T(8,128)S(1)}, u32[]{:S(2)}, u32[]{:S(2)}) collective-permute-start(f32[1536,128]{1,0:T(8,128)S(1)} %bitcast.10), channel_id=1, source_target_pairs={{0,64},{64,0},{1,65},{65,1},{2,66},{66,2},{3,67},{67,3},{4,68},{68... | collective-permute-start | bytes 2359304 | tf_op jit(solution)/shard_map/ppermute | solution.py:324

commit v5 on v4

--- a/solution.py
+++ b/solution.py
@@ -11,11 +11,11 @@
 ITERS = 3
 PAIRS = 4
 SAMPLES = 8
-IN = 21
-ROWS = 24
+ROWS = 21
+HELD = 24
 SHRINK = 2.0**-10
 VMEM = 48 * 1024 * 1024
-FULL = 60 * 1024 * 1024
+FULL = 57 * 1024 * 1024
 
 
 def shift_up(v, first):
@@ -139,7 +139,7 @@
 
 def pack_kernel(
     code, mean_all, draws_all, mask_all, noise_all, data_all, out,
-    mean, draws, mask, noise, data, sems, *, count, members,
+    mean, draws, mask, noise, data, sems, *, count, members, copies, lines,
 ):
     first = pl.multiple_of((code[0] % members) * count, count)
     mine = pl.ds(first, count)
@@ -159,12 +159,19 @@
         load.start()
     for load in loads:
         load.wait()
+
+    def place(r, rows):
+        for fy in range(count // lines):
+            for c in range(copies):
+                first_block = (fy * copies + c) * lines
+                out[pl.ds(first_block * ROWS + r, lines, stride=ROWS), :] = rows[fy * lines : fy * lines + lines]
+
     for a in range(1 + PAIRS):
         for p in range(2):
             for h in range(2):
                 lanes = slice(h * 128, h * 128 + 128)
                 rows = mean[p, :, lanes] if a == 0 else draws[a - 1, p, :, lanes]
-                out[pl.ds(a * 4 + p * 2 + h, count, stride=IN), :] = rows
+                place(a * 4 + p * 2 + h, rows)
     row = lax.broadcasted_iota(jnp.int32, (count, 128), 0)
     lane = lax.broadcasted_iota(jnp.int32, (count, 128), 1)
     chosen = lane == row + first
@@ -174,15 +181,15 @@
         for p in range(2):
             picked = jnp.sum(jnp.where(chosen, values[p : p + 1, :], 0.0), axis=1, keepdims=True)
             extra = jnp.where(lane == n * 2 + p, picked, extra)
-    out[pl.ds(20, count, stride=IN), :] = extra
+    place(20, extra)
 
 
 def plane_rows(ref, a, p, n):
-    return jnp.concatenate([ref[pl.ds(a * 4 + p * 2 + h, n, stride=IN), :] for h in range(2)], axis=1)
+    return jnp.concatenate([ref[pl.ds(a * 4 + p * 2 + h, n, stride=ROWS), :] for h in range(2)], axis=1)
 
 
 def columns(ref, n):
-    extra = ref[pl.ds(20, n, stride=IN), :]
+    extra = ref[pl.ds(20, n, stride=ROWS), :]
     spread = [jnp.broadcast_to(extra[:, c : c + 1], extra.shape) for c in range(4)]
     return spread[:2], spread[2:]
 
@@ -216,14 +223,14 @@
     for a, v in enumerate([latent] + basis):
         for p in range(2):
             for h in range(2):
-                block[pl.ds(a * 4 + p * 2 + h, n, stride=ROWS), :] = v[p][:, h * 128 : h * 128 + 128]
-    chunk = lines * ROWS
+                block[pl.ds(a * 4 + p * 2 + h, n, stride=HELD), :] = v[p][:, h * 128 : h * 128 + 128]
     for fy in range(groups):
-        start = pl.multiple_of(fy * (n // groups) * ROWS + (code[0] // members) * chunk, 8)
-        out[pl.ds(fy * chunk, chunk), :] = block[pl.ds(start, chunk), :]
+        for zl in range(lines):
+            start = (fy * (n // groups) + zl) * HELD + (code[0] // members) * (lines * HELD)
+            to = (fy * lines + zl) * ROWS
+            out[pl.ds(to, ROWS - 1), :] = block[pl.ds(pl.multiple_of(start, 8), ROWS - 1), :]
     row = jnp.broadcast_to(moments_row(basis), (groups * lines, 128))
-    for r in range(20, ROWS):
-        out[pl.ds(r, groups * lines, stride=ROWS), :] = row
+    out[pl.ds(ROWS - 1, groups * lines, stride=ROWS), :] = row
 
 
 def last_kernel(code, found, other, mean_final, cg_residual, *, chips, count):
@@ -271,8 +278,8 @@
     code = code.astype(jnp.int32).reshape(1)
 
     packed = pl.pallas_call(
-        functools.partial(pack_kernel, count=count, members=members),
-        out_shape=f32((lines * IN, 128)),
+        functools.partial(pack_kernel, count=count, members=members, copies=nzq, lines=nzl),
+        out_shape=f32((fields * ROWS, 128)),
         in_specs=[scalar] + [pl.BlockSpec(memory_space=pltpu.HBM)] * 5,
         out_specs=whole,
         scratch_shapes=[
@@ -287,9 +294,8 @@
         name="pack",
     )(code, mean_start, sample_draws, sight_mask, noise_weight, data)
 
-    packed = jnp.broadcast_to(packed.reshape(nfy, 1, nzl * IN, 1, 128), (nfy, nzq, nzl * IN, 1, 128))
-    packed = lax.all_to_all(packed.reshape(fields * IN, 1, 128), ("fy", "zq", "zl"), 0, 0, tiled=True)
-    packed = packed.reshape(fields * IN, 128)
+    packed = lax.all_to_all(packed.reshape(fields * ROWS, 1, 128), ("fy", "zq", "zl"), 0, 0, tiled=True)
+    packed = packed.reshape(fields * ROWS, 128)
 
     sharers = members * lines
     sums, factors, held = pl.pallas_call(
@@ -306,7 +312,7 @@
     )(packed, kernel)
 
     sums = jnp.broadcast_to(sums[None], (sharers, 1, 128))
-    sums = lax.all_to_all(sums, ("fy", "zl", "x", "core"), 0, 0, tiled=True)
+    sums = lax.all_to_all(sums, ("core", "x", "fy", "zl"), 0, 0, tiled=True)
     sums = sums.reshape(sharers, 128)
 
     found = pl.pallas_call(
@@ -314,13 +320,13 @@
         out_shape=f32((lines * ROWS, 128)),
         in_specs=[scalar] + [whole] * 5,
         out_specs=whole,
-        scratch_shapes=[pltpu.VMEM((fields * ROWS, 128), jnp.float32)],
+        scratch_shapes=[pltpu.VMEM((fields * HELD, 128), jnp.float32)],
         compiler_params=params,
         name="second",
     )(code, sums, packed, kernel, factors, held)
 
-    found = lax.all_to_all(found.reshape(lines, ROWS, 128), ("fy", "zl"), 0, 0, tiled=True)
-    found = spread(found.reshape(lines * ROWS, 128), "x").reshape(nx * lines * ROWS, 128)
+    found = lax.all_to_all(found.reshape(lines * ROWS, 1, 128), ("fy", "zl"), 0, 0, tiled=True)
+    found = spread(found, "x").reshape(nx * lines * ROWS, 128)
     other = lax.ppermute(found, "core", [(0, 1), (1, 0)])
 
     return pl.pallas_call(

time: 115 us -> 113 us (0.983)
  no operation moved by 1% of the time
where the time goes in v5:
time: 113 us
  blocking collectives  98.7 us (87%)
  Pallas kernels  6.04 us (5%)
  starting transfers between devices  5.31 us (5%)
  waiting for transfers between devices  1.75 us (2%)
    all_to_all x1, blocking collectives, local(): lax.all_to_all(packed.reshape(fields * ROWS, 1, 128), ('fy', 'zq', 'zl'),...  55.1 us
    all_to_all x1, blocking collectives, local(): sums = lax.all_to_all(sums, ('core', 'x', 'fy', 'zl'), 0, 0, tiled=True)  22.1 us
    all_to_all x1, blocking collectives, spread(): return lax.all_to_all(block, axis, 0, 0, tiled=True)  11.1 us
    all_to_all x1, blocking collectives, local(): lax.all_to_all(found.reshape(lines * ROWS, 1, 128), ('fy', 'zl'), 0, 0, t...  10.3 us
    ppermute x1, starting transfers between devices, local(): other = lax.ppermute(found, 'core', [(0, 1), (1, 0)])  5.31 us
  transfers between devices with their start and end apart: 1, of which 1 were waited for; matrix products, arithmetic and copies ran while one was open for 0% of the time, Pallas kernels for 0%

profile of v5, /device:TPU:1, one launch (start us, length us, event | category | flops | bytes accessed | tf_op | source)
XLA Modules:
  0.0 112.5 jit_solution(11637955008619300675)
XLA Ops:
  0.6 1.9 %pack.1 = f32[1344,128]{1,0:T(8,128)} custom-call(s32[1]{0:T(128)} %bitcast.code, f32[2,128,256]{2,1,0:T(8,128)} %mean_all.1, f32[4,2,128,256]{3,2,1,0:T(8,128)} %draws_all.1, s32[2,128]{1,0:T(2,128)} %mask_all.1, f32[2,128]{1,0:T(2,128)} %noise_all.1, f32[2,128]{1,0:T(2,128)} %data_all.1), custom_call_target="tpu_custom_call" | custom-call | tf_op jit(solution)/shard_map/pack/pallas_call | solution.py:280
  2.6 0.0 copy-start
  2.6 55.1 %all_to_all.20 = f32[1344,1,128]{2,1,0:T(1,128)S(1)} all-to-all(f32[1344,1,128]{2,1,0:T(1,128)} %bitcast.19), channel_id=1, replica_groups=mesh['x'=4,'core'=2,'fy'=4,'zq'=4,'zl'=4] {'fy','zq','zl'}, dimensions={0} | all-to-all | bytes 1376256 | tf_op jit(solution)/shard_map/all_to_all | solution.py:297
  57.7 0.0 copy-done
  57.7 1.5 %first.1 = (f32[1,128]{1,0:T(1,128)S(1)}, f32[8,2,64,256]{3,2,1,0:T(8,128)S(1)}, f32[4,2,64,256]{3,2,1,0:T(8,128)S(1)}) custom-call(f32[1344,128]{1,0:T(8,128)S(1)} %bitcast.12, f32[3,256]{1,0:T(4,128)S(1)} %copy-done), custom_call_target="tpu_custom_call" | custom-call | tf_op jit(solution)/shard_map/first/pallas_call | solution.py:301
  59.2 22.1 %all_to_all.21 = f32[128,1,128]{2,1,0:T(1,128)S(1)} all-to-all(f32[128,1,128]{2,1,0:T(1,128)S(1)} %broadcast_in_dim.17), channel_id=1, replica_groups=mesh['x'=4,'core'=2,'fy'=4,'zq'=4,'zl'=4] {'core','x','fy','zl'}, dimensions={0} | all-to-all | bytes 131072 | tf_op jit(solution)/shard_map/all_to_all | solution.py:315
  81.3 1.5 %second.1 = f32[336,128]{1,0:T(8,128)S(1)} custom-call(s32[1]{0:T(128)} %bitcast.code, f32[128,128]{1,0:T(8,128)S(1)} %bitcast.17, f32[1344,128]{1,0:T(8,128)S(1)} %bitcast.13, f32[3,256]{1,0:T(4,128)S(1)} %copy-done, f32[8,2,64,256]{3,2,1,0:T(8,128)S(1)} %get-tuple-element.6.factors, f32[4,2,64,256]{3,2,1,0:T(8,128)S(1)} %get-tuple-element.7.held), custom_call_target="tpu_custom_call" | custom-call | tf_op jit(solution)/shard_map/second/pallas_call | solution.py:318
  82.8 10.3 %all_to_all.22 = f32[336,1,128]{2,1,0:T(1,128)S(1)} all-to-all(f32[336,1,128]{2,1,0:T(1,128)S(1)} %bitcast.16), channel_id=1, replica_groups=mesh['x'=4,'core'=2,'fy'=4,'zq'=4,'zl'=4] {'fy','zl'}, dimensions={0} | all-to-all | bytes 344064 | tf_op jit(solution)/shard_map/all_to_all | solution.py:328
  93.2 11.1 %all_to_all.23 = f32[4,336,1,128]{3,1,2,0:T(8,128)S(1)} all-to-all(f32[4,336,1,128]{3,1,2,0:T(8,128)S(1)} %broadcast_in_dim.19), channel_id=1, replica_groups=mesh['x'=4,'core'=2,'fy'=4,'zq'=4,'zl'=4] {'x'}, dimensions={0} | all-to-all | bytes 1376256 | tf_op jit(solution)/shard_map/all_to_all | solution.py:263
  104.4 5.3 %collective-permute-start = (f32[1344,128]{1,0:T(8,128)S(1)}, f32[1344,128]{1,0:T(8,128)S(1)}, u32[]{:S(2)}, u32[]{:S(2)}) collective-permute-start(f32[1344,128]{1,0:T(8,128)S(1)} %bitcast.14), channel_id=1, source_target_pairs={{0,64},{64,0},{1,65},{65,1},{2,66},{66,2},{3,67},{67,3},{4,68},{68... | collective-permute-start | bytes 2064392 | tf_op jit(solution)/shard_map/ppermute | solution.py:330
  109.7 1.7 %collective-permute-done.other = f32[1344,128]{1,0:T(8,128)S(1)} collective-permute-done((f32[1344,128]{1,0:T(8,128)S(1)}, f32[1344,128]{1,0:T(8,128)S(1)}, u32[]{:S(2)}, u32[]{:S(2)}) %collective-permute-start) | collective-permute-done | bytes 688160 | tf_op jit(solution)/shard_map/ppermute | solution.py:330
  111.5 1.1 last.1
  (2 shorter events, 0.1 us)
Async XLA Ops:
  2.6 55.1 %copy-start = (f32[3,256]{1,0:T(4,128)S(1)}, f32[3,256]{1,0:T(4,128)}, u32[]{:S(2)}) copy-start(f32[3,256]{1,0:T(4,128)} %kernel.3) | copy-start | bytes 9220
  104.4 7.1 %collective-permute-start = (f32[1344,128]{1,0:T(8,128)S(1)}, f32[1344,128]{1,0:T(8,128)S(1)}, u32[]{:S(2)}, u32[]{:S(2)}) collective-permute-start(f32[1344,128]{1,0:T(8,128)S(1)} %bitcast.14), channel_id=1, source_target_pairs={{0,64},{64,0},{1,65},{65,1},{2,66},{66,2},{3,67},{67,3},{4,68},{68... | collective-permute-start | bytes 2064392 | tf_op jit(solution)/shard_map/ppermute | solution.py:330

commit v6 on v5

--- a/solution.py
+++ b/solution.py
@@ -82,18 +82,67 @@
     return row
 
 
-def coefficients(row):
+def two_sum(a, b):
+    total = a + b
+    part = total - a
+    return total, (a - (total - part)) + (b - part)
+
+
+def halves_of(a):
+    scaled = a * 4097.0
+    high = scaled - (scaled - a)
+    return high, a - high
+
+
+def two_product(a, b):
+    product = a * b
+    (ah, al), (bh, bl) = halves_of(a), halves_of(b)
+    return product, ((ah * bh - product) + ah * bl + al * bh) + al * bl
+
+
+def careful_sum(rows):
+    total, rest = rows[:8], jnp.zeros((8, 128), jnp.float32)
+    for t in range(8, rows.shape[0], 8):
+        total, error = two_sum(total, rows[t : t + 8])
+        rest = rest + error
+    for shift in (4, 2, 1):
+        other, other_rest = pltpu.roll(total, shift, 0), pltpu.roll(rest, shift, 0)
+        total, error = two_sum(total, other)
+        rest = rest + other_rest + error
+    return total[:1], rest[:1]
+
+
+def coefficients(rows):
     lane = lax.broadcasted_iota(jnp.int32, (1, 128), 1)
-    nu = [jnp.sum(jnp.where(lane == n, row, 0.0), axis=1, keepdims=True) for n in range(2 * ITERS)]
+    total, rest = careful_sum(rows)
+    nu = [
+        tuple(jnp.sum(jnp.where(lane == n, part, 0.0), axis=1, keepdims=True) for part in (total, rest))
+        for n in range(2 * ITERS)
+    ]
     zero, one = jnp.zeros((1, 1), jnp.float32), jnp.ones((1, 1), jnp.float32)
 
     def inner(a, b):
-        total = zero
+        weights = {}
         for i, x in enumerate(a):
             for j, y in enumerate(b):
                 if i + j < 2 * ITERS:
-                    total = total + x * y * nu[i + j]
-        return total
+                    product, error = two_product(x, y)
+                    if i + j in weights:
+                        high, low = weights[i + j]
+                        high, more = two_sum(high, product)
+                        weights[i + j] = high, low + (error + more)
+                    else:
+                        weights[i + j] = product, error
+        total, rest = None, zero
+        for n, (high, low) in weights.items():
+            product, error = two_product(high, nu[n][0])
+            error = error + (high * nu[n][1] + low * nu[n][0])
+            if total is None:
+                total, rest = product, error
+            else:
+                total, more = two_sum(total, product)
+                rest = rest + (error + more)
+        return total + rest
 
     def ratio(a, b):
         return jnp.where(b > 0.0, a / jnp.where(b > 0.0, b, 1.0), 0.0)
@@ -101,15 +150,15 @@
     residual = [one]
     direction = [one]
     step = [zero] * ITERS
-    norm_now = nu[0]
+    norm_now = nu[0][0] + nu[0][1]
     for it in range(ITERS):
         padded = direction + [zero]
         image = [padded[0]] + [padded[j] + (1.0 / SHRINK) * padded[j - 1] for j in range(1, len(padded))]
-        alpha = ratio(norm_now, inner(direction, image))
+        alpha = jnp.clip(ratio(norm_now, inner(direction, image)), 0.0, 1.0)
         step = [s + alpha * direction[j] if j < len(direction) else s for j, s in enumerate(step)]
         residual = [r - alpha * i for r, i in zip(residual + [zero], image)]
         if it < ITERS - 1:
-            norm_next = inner(residual, residual)
+            norm_next = jnp.maximum(inner(residual, residual), 0.0)
             beta = ratio(norm_next, norm_now)
             direction = [r + beta * d for r, d in zip(residual, direction + [zero])]
             norm_now = norm_next
@@ -215,7 +264,7 @@
 def second_kernel(code, sums, packed, kernel, factors, held, out, block, *, n, groups, lines, members):
     taps = [kernel[t : t + 1, :] for t in range(3)]
     ends = edges((n, 256))
-    step, _ = coefficients(jnp.sum(sums[...], axis=0, keepdims=True))
+    step, _ = coefficients(sums[...])
     basis = [tuple(held[j, p] for p in range(2)) for j in range(1 + ITERS)]
     latent = combine([jnp.ones((1, 1), jnp.float32)] + step, basis)
     weight, offset = columns(packed, n)
@@ -236,8 +285,8 @@
 def last_kernel(code, found, other, mean_final, cg_residual, *, chips, count):
     core = code[0] % 2
     n = chips * count
-    sums = found[pl.ds(20, n, stride=ROWS), :] + other[pl.ds(20, n, stride=ROWS), :]
-    step, residual = coefficients(jnp.sum(sums, axis=0, keepdims=True))
+    sums = [ref[pl.ds(20, n, stride=ROWS), :] for ref in (found, other)]
+    step, residual = coefficients(jnp.concatenate(sums, axis=0))
     for ref, owner in ((found, core), (other, 1 - core)):
         for x in range(chips):
             rows = pl.ds(pl.multiple_of((2 * x + owner) * count, count), count)

time: 113 us -> 113 us (level)
  no operation moved by 1% of the time
where the time goes in v6:
time: 113 us
  blocking collectives  98.7 us (87%)
  Pallas kernels  6.29 us (6%)
  starting transfers between devices  5.31 us (5%)
  waiting for transfers between devices  1.75 us (2%)
    all_to_all x1, blocking collectives, local(): lax.all_to_all(packed.reshape(fields * ROWS, 1, 128), ('fy', 'zq', 'zl'),...  55.1 us
    all_to_all x1, blocking collectives, local(): sums = lax.all_to_all(sums, ('core', 'x', 'fy', 'zl'), 0, 0, tiled=True)  22.1 us
    all_to_all x1, blocking collectives, spread(): return lax.all_to_all(block, axis, 0, 0, tiled=True)  11.1 us
    all_to_all x1, blocking collectives, local(): lax.all_to_all(found.reshape(lines * ROWS, 1, 128), ('fy', 'zl'), 0, 0, t...  10.3 us
    ppermute x1, starting transfers between devices, local(): other = lax.ppermute(found, 'core', [(0, 1), (1, 0)])  5.31 us
  transfers between devices with their start and end apart: 1, of which 1 were waited for; matrix products, arithmetic and copies ran while one was open for 0% of the time, Pallas kernels for 0%

profile of v6, /device:TPU:1, one launch (start us, length us, event | category | flops | bytes accessed | tf_op | source)
XLA Modules:
  0.0 112.8 jit_solution(9468824216492213866)
XLA Ops:
  0.6 1.9 %pack.1 = f32[1344,128]{1,0:T(8,128)} custom-call(s32[1]{0:T(128)} %bitcast.code, f32[2,128,256]{2,1,0:T(8,128)} %mean_all.1, f32[4,2,128,256]{3,2,1,0:T(8,128)} %draws_all.1, s32[2,128]{1,0:T(2,128)} %mask_all.1, f32[2,128]{1,0:T(2,128)} %noise_all.1, f32[2,128]{1,0:T(2,128)} %data_all.1), custom_call_target="tpu_custom_call" | custom-call | tf_op jit(solution)/shard_map/pack/pallas_call | solution.py:329
  2.6 0.0 copy-start
  2.6 55.1 %all_to_all.20 = f32[1344,1,128]{2,1,0:T(1,128)S(1)} all-to-all(f32[1344,1,128]{2,1,0:T(1,128)} %bitcast.19), channel_id=1, replica_groups=mesh['x'=4,'core'=2,'fy'=4,'zq'=4,'zl'=4] {'fy','zq','zl'}, dimensions={0} | all-to-all | bytes 1376256 | tf_op jit(solution)/shard_map/all_to_all | solution.py:346
  57.7 0.0 copy-done
  57.7 1.5 %first.1 = (f32[1,128]{1,0:T(1,128)S(1)}, f32[8,2,64,256]{3,2,1,0:T(8,128)S(1)}, f32[4,2,64,256]{3,2,1,0:T(8,128)S(1)}) custom-call(f32[1344,128]{1,0:T(8,128)S(1)} %bitcast.12, f32[3,256]{1,0:T(4,128)S(1)} %copy-done), custom_call_target="tpu_custom_call" | custom-call | tf_op jit(solution)/shard_map/first/pallas_call | solution.py:350
  59.2 22.1 %all_to_all.21 = f32[128,1,128]{2,1,0:T(1,128)S(1)} all-to-all(f32[128,1,128]{2,1,0:T(1,128)S(1)} %broadcast_in_dim.17), channel_id=1, replica_groups=mesh['x'=4,'core'=2,'fy'=4,'zq'=4,'zl'=4] {'core','x','fy','zl'}, dimensions={0} | all-to-all | bytes 131072 | tf_op jit(solution)/shard_map/all_to_all | solution.py:364
  81.3 1.7 %second.1 = f32[336,128]{1,0:T(8,128)S(1)} custom-call(s32[1]{0:T(128)} %bitcast.code, f32[128,128]{1,0:T(8,128)S(1)} %bitcast.17, f32[1344,128]{1,0:T(8,128)S(1)} %bitcast.13, f32[3,256]{1,0:T(4,128)S(1)} %copy-done, f32[8,2,64,256]{3,2,1,0:T(8,128)S(1)} %get-tuple-element.6.factors, f32[4,2,64,256]{3,2,1,0:T(8,128)S(1)} %get-tuple-element.7.held), custom_call_target="tpu_custom_call" | custom-call | tf_op jit(solution)/shard_map/second/pallas_call | solution.py:367
  83.0 10.3 %all_to_all.22 = f32[336,1,128]{2,1,0:T(1,128)S(1)} all-to-all(f32[336,1,128]{2,1,0:T(1,128)S(1)} %bitcast.16), channel_id=1, replica_groups=mesh['x'=4,'core'=2,'fy'=4,'zq'=4,'zl'=4] {'fy','zl'}, dimensions={0} | all-to-all | bytes 344064 | tf_op jit(solution)/shard_map/all_to_all | solution.py:377
  93.4 11.1 %all_to_all.23 = f32[4,336,1,128]{3,1,2,0:T(8,128)S(1)} all-to-all(f32[4,336,1,128]{3,1,2,0:T(8,128)S(1)} %broadcast_in_dim.19), channel_id=1, replica_groups=mesh['x'=4,'core'=2,'fy'=4,'zq'=4,'zl'=4] {'x'}, dimensions={0} | all-to-all | bytes 1376256 | tf_op jit(solution)/shard_map/all_to_all | solution.py:312
  104.5 5.3 %collective-permute-start = (f32[1344,128]{1,0:T(8,128)S(1)}, f32[1344,128]{1,0:T(8,128)S(1)}, u32[]{:S(2)}, u32[]{:S(2)}) collective-permute-start(f32[1344,128]{1,0:T(8,128)S(1)} %bitcast.14), channel_id=1, source_target_pairs={{0,64},{64,0},{1,65},{65,1},{2,66},{66,2},{3,67},{67,3},{4,68},{68... | collective-permute-start | bytes 2064392 | tf_op jit(solution)/shard_map/ppermute | solution.py:379
  109.8 1.7 %collective-permute-done.other = f32[1344,128]{1,0:T(8,128)S(1)} collective-permute-done((f32[1344,128]{1,0:T(8,128)S(1)}, f32[1344,128]{1,0:T(8,128)S(1)}, u32[]{:S(2)}, u32[]{:S(2)}) %collective-permute-start) | collective-permute-done | bytes 688160 | tf_op jit(solution)/shard_map/ppermute | solution.py:379
  111.6 1.2 %last.1 = (f32[2,128,256]{2,1,0:T(8,128)}, f32[2,128,256]{2,1,0:T(8,128)}) custom-call(s32[1]{0:T(128)} %bitcast.code, f32[1344,128]{1,0:T(8,128)S(1)} %bitcast.15, f32[1344,128]{1,0:T(8,128)S(1)} %collective-permute-done.other), custom_call_target="tpu_custom_call" | custom-call | tf_op jit(solution)/shard_map/last/pallas_call | solution.py:381
  (2 shorter events, 0.1 us)
Async XLA Ops:
  2.6 55.1 %copy-start = (f32[3,256]{1,0:T(4,128)S(1)}, f32[3,256]{1,0:T(4,128)}, u32[]{:S(2)}) copy-start(f32[3,256]{1,0:T(4,128)} %kernel.3) | copy-start | bytes 9220
  104.5 7.1 %collective-permute-start = (f32[1344,128]{1,0:T(8,128)S(1)}, f32[1344,128]{1,0:T(8,128)S(1)}, u32[]{:S(2)}, u32[]{:S(2)}) collective-permute-start(f32[1344,128]{1,0:T(8,128)S(1)} %bitcast.14), channel_id=1, source_target_pairs={{0,64},{64,0},{1,65},{65,1},{2,66},{66,2},{3,67},{67,3},{4,68},{68... | collective-permute-start | bytes 2064392 | tf_op jit(solution)/shard_map/ppermute | solution.py:379

commit v7 on v6

--- a/solution.py
+++ b/solution.py
@@ -188,7 +188,7 @@
 
 def pack_kernel(
     code, mean_all, draws_all, mask_all, noise_all, data_all, out,
-    mean, draws, mask, noise, data, sems, *, count, members, copies, lines,
+    mean, draws, mask, noise, data, sems, *, count, members, halves, copies, lines,
 ):
     first = pl.multiple_of((code[0] % members) * count, count)
     mine = pl.ds(first, count)
@@ -210,10 +210,13 @@
         load.wait()
 
     def place(r, rows):
-        for fy in range(count // lines):
-            for c in range(copies):
-                first_block = (fy * copies + c) * lines
-                out[pl.ds(first_block * ROWS + r, lines, stride=ROWS), :] = rows[fy * lines : fy * lines + lines]
+        groups = count // lines
+        width = halves * groups
+        for c in range(copies):
+            for h in range(halves):
+                for fy in range(groups):
+                    to = c * lines * width + h * groups + fy
+                    out[pl.ds(to * ROWS + r, lines, stride=width * ROWS), :] = rows[fy * lines : fy * lines + lines]
 
     for a in range(1 + PAIRS):
         for p in range(2):
@@ -233,26 +236,39 @@
     place(20, extra)
 
 
-def plane_rows(ref, a, p, n):
-    return jnp.concatenate([ref[pl.ds(a * 4 + p * 2 + h, n, stride=ROWS), :] for h in range(2)], axis=1)
-
-
-def columns(ref, n):
-    extra = ref[pl.ds(20, n, stride=ROWS), :]
+def lane_rows(ref, r, order):
+    halves, groups, run = order
+    width = halves * groups
+    return jnp.concatenate(
+        [
+            ref[pl.ds((h * groups + fy) * ROWS + r, run, stride=width * ROWS), :]
+            for fy in range(groups)
+            for h in range(halves)
+        ],
+        axis=0,
+    )
+
+
+def plane_rows(ref, a, p, order):
+    return jnp.concatenate([lane_rows(ref, a * 4 + p * 2 + h, order) for h in range(2)], axis=1)
+
+
+def columns(ref, order):
+    extra = lane_rows(ref, 20, order)
     spread = [jnp.broadcast_to(extra[:, c : c + 1], extra.shape) for c in range(4)]
     return spread[:2], spread[2:]
 
 
-def first_kernel(packed, kernel, sums, factors, held, *, n):
+def first_kernel(packed, kernel, sums, factors, held, *, n, order):
     taps = [kernel[t : t + 1, :] for t in range(3)]
     ends = edges((n, 256))
-    latent = tuple(plane_rows(packed, 0, p, n) for p in range(2))
+    latent = tuple(plane_rows(packed, 0, p, order) for p in range(2))
     for k in range(PAIRS):
-        spread = refine(tuple(plane_rows(packed, 1 + k, p, n) for p in range(2)), taps, ends)
+        spread = refine(tuple(plane_rows(packed, 1 + k, p, order) for p in range(2)), taps, ends)
         for p in range(2):
             factors[2 * k, p] = jnp.exp(spread[p])
             factors[2 * k + 1, p] = jnp.exp(-spread[p])
-    weight, offset = columns(packed, n)
+    weight, offset = columns(packed, order)
     basis = krylov(latent, factors, weight, offset, taps, ends)
     for p in range(2):
         held[0, p] = latent[p]
@@ -261,13 +277,13 @@
     sums[...] = moments_row(basis)
 
 
-def second_kernel(code, sums, packed, kernel, factors, held, out, block, *, n, groups, lines, members):
+def second_kernel(code, sums, packed, kernel, factors, held, out, block, *, n, order, groups, lines, members):
     taps = [kernel[t : t + 1, :] for t in range(3)]
     ends = edges((n, 256))
     step, _ = coefficients(sums[...])
     basis = [tuple(held[j, p] for p in range(2)) for j in range(1 + ITERS)]
     latent = combine([jnp.ones((1, 1), jnp.float32)] + step, basis)
-    weight, offset = columns(packed, n)
+    weight, offset = columns(packed, order)
     basis = krylov(latent, factors, weight, offset, taps, ends)
     for a, v in enumerate([latent] + basis):
         for p in range(2):
@@ -313,9 +329,9 @@
 
 
 def local(mean_start, sample_draws, kernel, sight_mask, noise_weight, data):
-    nx, nc, nfy, nzq, nzl = (lax.axis_size(a) for a in ("x", "core", "fy", "zq", "zl"))
+    nx, nc, nfy, nzh, nzk, nzl = (lax.axis_size(a) for a in ("x", "core", "fy", "zh", "zk", "zl"))
     members = nx * nc
-    fields = nfy * nzq * nzl
+    fields = nfy * nzh * nzk * nzl
     lines = nfy * nzl
     count = mean_start.shape[1] // members
     depth = mean_start.shape[2]
@@ -323,11 +339,11 @@
     params = pltpu.CompilerParams(vmem_limit_bytes=VMEM)
     whole = pl.BlockSpec(memory_space=pltpu.VMEM)
     scalar = pl.BlockSpec(memory_space=pltpu.SMEM)
-    code = lax.axis_index("zq") * members + lax.axis_index("x") * nc + lax.axis_index("core")
+    code = lax.axis_index(("zh", "zk")) * members + lax.axis_index("x") * nc + lax.axis_index("core")
     code = code.astype(jnp.int32).reshape(1)
 
     packed = pl.pallas_call(
-        functools.partial(pack_kernel, count=count, members=members, copies=nzq, lines=nzl),
+        functools.partial(pack_kernel, count=count, members=members, halves=nzh, copies=nzk, lines=nzl),
         out_shape=f32((fields * ROWS, 128)),
         in_specs=[scalar] + [pl.BlockSpec(memory_space=pltpu.HBM)] * 5,
         out_specs=whole,
@@ -343,12 +359,13 @@
         name="pack",
     )(code, mean_start, sample_draws, sight_mask, noise_weight, data)
 
-    packed = lax.all_to_all(packed.reshape(fields * ROWS, 1, 128), ("fy", "zq", "zl"), 0, 0, tiled=True)
+    packed = lax.all_to_all(packed.reshape(fields * ROWS, 1, 128), ("zk", "zl", "zh", "fy"), 0, 0, tiled=True)
     packed = packed.reshape(fields * ROWS, 128)
 
+    order = (nzh, nfy, nzk * nzl)
     sharers = members * lines
     sums, factors, held = pl.pallas_call(
-        functools.partial(first_kernel, n=fields),
+        functools.partial(first_kernel, n=fields, order=order),
         out_shape=[
             f32((1, 128)),
             f32((SAMPLES, 2, fields, depth)),
@@ -365,7 +382,7 @@
     sums = sums.reshape(sharers, 128)
 
     found = pl.pallas_call(
-        functools.partial(second_kernel, n=fields, groups=nfy, lines=nzl, members=members),
+        functools.partial(second_kernel, n=fields, order=order, groups=nfy, lines=nzl, members=members),
         out_shape=f32((lines * ROWS, 128)),
         in_specs=[scalar] + [whole] * 5,
         out_specs=whole,
@@ -389,8 +406,8 @@
 
 
 def solution(mesh):
-    split = Mesh(mesh.devices.reshape(4, 2, 4, 4, 4), ("x", "core", "fy", "zq", "zl"))
-    field = ("fy", "zq", "zl")
+    split = Mesh(mesh.devices.reshape(4, 2, 4, 2, 2, 4), ("x", "core", "fy", "zh", "zk", "zl"))
+    field = ("fy", "zh", "zk", "zl")
     placed = (
         P(field, None, None),
         P(None, field, None, None),

time: 113 us -> 113 us (level)
    all_to_all x1, blocking collectives: 55.1 us -> 56.8 us  [local(): lax.all_to_all(packed.reshape(fields * ROWS, 1, 128), ('zk', 'zl', 'zh',...]
    all_to_all x1, blocking collectives: 22.1 us -> 20.6 us  [local(): sums = lax.all_to_all(sums, ('core', 'x', 'fy', 'zl'), 0, 0, tiled=True)]
where the time goes in v7:
time: 113 us
  blocking collectives  98.9 us (88%)
  Pallas kernels  6.3 us (6%)
  starting transfers between devices  5.31 us (5%)
  waiting for transfers between devices  1.75 us (2%)
    all_to_all x1, blocking collectives, local(): lax.all_to_all(packed.reshape(fields * ROWS, 1, 128), ('zk', 'zl', 'zh',...  56.8 us
    all_to_all x1, blocking collectives, local(): sums = lax.all_to_all(sums, ('core', 'x', 'fy', 'zl'), 0, 0, tiled=True)  20.6 us
    all_to_all x1, blocking collectives, spread(): return lax.all_to_all(block, axis, 0, 0, tiled=True)  11.1 us
    all_to_all x1, blocking collectives, local(): lax.all_to_all(found.reshape(lines * ROWS, 1, 128), ('fy', 'zl'), 0, 0, t...  10.3 us
    ppermute x1, starting transfers between devices, local(): other = lax.ppermute(found, 'core', [(0, 1), (1, 0)])  5.31 us
  transfers between devices with their start and end apart: 1, of which 1 were waited for; matrix products, arithmetic and copies ran while one was open for 0% of the time, Pallas kernels for 0%

profile of v7, /device:TPU:1, one launch (start us, length us, event | category | flops | bytes accessed | tf_op | source)
XLA Modules:
  0.0 113.1 jit_solution(14734086948130597827)
XLA Ops:
  0.6 1.9 %pack.1 = f32[1344,128]{1,0:T(8,128)} custom-call(s32[1]{0:T(128)} %bitcast.code, f32[2,128,256]{2,1,0:T(8,128)} %mean_all.1, f32[4,2,128,256]{3,2,1,0:T(8,128)} %draws_all.1, s32[2,128]{1,0:T(2,128)} %mask_all.1, f32[2,128]{1,0:T(2,128)} %noise_all.1, f32[2,128]{1,0:T(2,128)} %data_all.1), custom_call_target="tpu_custom_call" | custom-call | tf_op jit(solution)/shard_map/pack/pallas_call | solution.py:345
  2.6 0.0 copy-start
  2.6 56.8 %all_to_all.20 = f32[1344,1,128]{2,1,0:T(1,128)S(1)} all-to-all(f32[1344,1,128]{2,1,0:T(1,128)} %bitcast.19), channel_id=1, replica_groups=mesh['x'=4,'core'=2,'fy'=4,'zh'=2,'zk'=2,'zl'=4] {'zk','zl','zh','fy'}, dimensions={0} | all-to-all | bytes 1376256 | tf_op jit(solution)/shard_map/all_to_all | solution.py:362
  59.4 0.0 copy-done
  59.4 1.5 %first.1 = (f32[1,128]{1,0:T(1,128)S(1)}, f32[8,2,64,256]{3,2,1,0:T(8,128)S(1)}, f32[4,2,64,256]{3,2,1,0:T(8,128)S(1)}) custom-call(f32[1344,128]{1,0:T(8,128)S(1)} %bitcast.12, f32[3,256]{1,0:T(4,128)S(1)} %copy-done), custom_call_target="tpu_custom_call" | custom-call | tf_op jit(solution)/shard_map/first/pallas_call | solution.py:367
  61.0 20.6 %all_to_all.21 = f32[128,1,128]{2,1,0:T(1,128)S(1)} all-to-all(f32[128,1,128]{2,1,0:T(1,128)S(1)} %broadcast_in_dim.17), channel_id=1, replica_groups=mesh['x'=4,'core'=2,'fy'=4,'zh'=2,'zk'=2,'zl'=4] {'core','x','fy','zl'}, dimensions={0} | all-to-all | bytes 131072 | tf_op jit(solution)/shard_map/all_to_all | solution.py:381
  81.6 1.6 %second.1 = f32[336,128]{1,0:T(8,128)S(1)} custom-call(s32[1]{0:T(128)} %bitcast.code, f32[128,128]{1,0:T(8,128)S(1)} %bitcast.17, f32[1344,128]{1,0:T(8,128)S(1)} %bitcast.13, f32[3,256]{1,0:T(4,128)S(1)} %copy-done, f32[8,2,64,256]{3,2,1,0:T(8,128)S(1)} %get-tuple-element.6.factors, f32[4,2,64,256]{3,2,1,0:T(8,128)S(1)} %get-tuple-element.7.held), custom_call_target="tpu_custom_call" | custom-call | tf_op jit(solution)/shard_map/second/pallas_call | solution.py:384
  83.2 10.3 %all_to_all.22 = f32[336,1,128]{2,1,0:T(1,128)S(1)} all-to-all(f32[336,1,128]{2,1,0:T(1,128)S(1)} %bitcast.16), channel_id=1, replica_groups=mesh['x'=4,'core'=2,'fy'=4,'zh'=2,'zk'=2,'zl'=4] {'fy','zl'}, dimensions={0} | all-to-all | bytes 344064 | tf_op jit(solution)/shard_map/all_to_all | solution.py:394
  93.6 11.1 %all_to_all.23 = f32[4,336,1,128]{3,1,2,0:T(8,128)S(1)} all-to-all(f32[4,336,1,128]{3,1,2,0:T(8,128)S(1)} %broadcast_in_dim.19), channel_id=1, replica_groups=mesh['x'=4,'core'=2,'fy'=4,'zh'=2,'zk'=2,'zl'=4] {'x'}, dimensions={0} | all-to-all | bytes 1376256 | tf_op jit(solution)/shard_map/all_to_all | solution.py:328
  104.8 5.3 %collective-permute-start = (f32[1344,128]{1,0:T(8,128)S(1)}, f32[1344,128]{1,0:T(8,128)S(1)}, u32[]{:S(2)}, u32[]{:S(2)}) collective-permute-start(f32[1344,128]{1,0:T(8,128)S(1)} %bitcast.14), channel_id=1, source_target_pairs={{0,64},{64,0},{1,65},{65,1},{2,66},{66,2},{3,67},{67,3},{4,68},{68... | collective-permute-start | bytes 2064392 | tf_op jit(solution)/shard_map/ppermute | solution.py:396
  110.1 1.7 %collective-permute-done.other = f32[1344,128]{1,0:T(8,128)S(1)} collective-permute-done((f32[1344,128]{1,0:T(8,128)S(1)}, f32[1344,128]{1,0:T(8,128)S(1)}, u32[]{:S(2)}, u32[]{:S(2)}) %collective-permute-start) | collective-permute-done | bytes 688160 | tf_op jit(solution)/shard_map/ppermute | solution.py:396
  111.9 1.2 %last.1 = (f32[2,128,256]{2,1,0:T(8,128)}, f32[2,128,256]{2,1,0:T(8,128)}) custom-call(s32[1]{0:T(128)} %bitcast.code, f32[1344,128]{1,0:T(8,128)S(1)} %bitcast.15, f32[1344,128]{1,0:T(8,128)S(1)} %collective-permute-done.other), custom_call_target="tpu_custom_call" | custom-call | tf_op jit(solution)/shard_map/last/pallas_call | solution.py:398
  (2 shorter events, 0.1 us)
Async XLA Ops:
  2.6 56.9 %copy-start = (f32[3,256]{1,0:T(4,128)S(1)}, f32[3,256]{1,0:T(4,128)}, u32[]{:S(2)}) copy-start(f32[3,256]{1,0:T(4,128)} %kernel.3) | copy-start | bytes 9220
  104.8 7.1 %collective-permute-start = (f32[1344,128]{1,0:T(8,128)S(1)}, f32[1344,128]{1,0:T(8,128)S(1)}, u32[]{:S(2)}, u32[]{:S(2)}) collective-permute-start(f32[1344,128]{1,0:T(8,128)S(1)} %bitcast.14), channel_id=1, source_target_pairs={{0,64},{64,0},{1,65},{65,1},{2,66},{66,2},{3,67},{67,3},{4,68},{68... | collective-permute-start | bytes 2064392 | tf_op jit(solution)/shard_map/ppermute | solution.py:396

commit v8 on v6

--- a/solution.py
+++ b/solution.py
@@ -293,7 +293,7 @@
             for p in range(2):
                 for h in range(2):
                     v = [
-                        ref[pl.ds(x * count * ROWS + a * 4 + p * 2 + h, count, stride=ROWS), :]
+                        ref[pl.ds(x * ROWS + a * 4 + p * 2 + h, count, stride=chips * ROWS), :]
                         for a in range(2 + ITERS)
                     ]
                     latent = v[0]
@@ -304,12 +304,6 @@
                         rest = rest + c * b
                     mean_final[p, rows, h * 128 : h * 128 + 128] = latent
                     cg_residual[p, rows, h * 128 : h * 128 + 128] = rest
-
-
-def spread(block, axis):
-    copies = lax.axis_size(axis)
-    block = jnp.broadcast_to(block[None], (copies,) + block.shape)
-    return lax.all_to_all(block, axis, 0, 0, tiled=True)
 
 
 def local(mean_start, sample_draws, kernel, sight_mask, noise_weight, data):
@@ -374,8 +368,9 @@
         name="second",
     )(code, sums, packed, kernel, factors, held)
 
-    found = lax.all_to_all(found.reshape(lines * ROWS, 1, 128), ("fy", "zl"), 0, 0, tiled=True)
-    found = spread(found, "x").reshape(nx * lines * ROWS, 128)
+    found = jnp.broadcast_to(found.reshape(lines, 1, ROWS, 1, 128), (lines, nx, ROWS, 1, 128))
+    found = lax.all_to_all(found.reshape(lines * nx * ROWS, 1, 128), ("fy", "zl", "x"), 0, 0, tiled=True)
+    found = found.reshape(nx * lines * ROWS, 128)
     other = lax.ppermute(found, "core", [(0, 1), (1, 0)])
 
     return pl.pallas_call(

time: 113 us -> 115 us (1.018)
  blocking collectives: 98.7 us -> 102 us
  starting transfers between devices: 5.31 us -> 4.04 us
    all_to_all x2 -> x1, blocking collectives: 21.5 us -> 24.8 us  [local(): lax.all_to_all(found.reshape(lines * nx * ROWS, 1, 128), ('fy', 'zl', 'x'...]
    ppermute x1, starting transfers between devices: 5.31 us -> 4.04 us  [local(): other = lax.ppermute(found, 'core', [(0, 1), (1, 0)])]
where the time goes in v8:
time: 115 us
  blocking collectives  102 us (89%)
  Pallas kernels  6.29 us (5%)
  starting transfers between devices  4.04 us (4%)
  waiting for transfers between devices  1.75 us (2%)
    all_to_all x1, blocking collectives, local(): lax.all_to_all(packed.reshape(fields * ROWS, 1, 128), ('fy', 'zq', 'zl'),...  55.1 us
    all_to_all x1, blocking collectives, local(): lax.all_to_all(found.reshape(lines * nx * ROWS, 1, 128), ('fy', 'zl', 'x'...  24.8 us
    all_to_all x1, blocking collectives, local(): sums = lax.all_to_all(sums, ('core', 'x', 'fy', 'zl'), 0, 0, tiled=True)  22.1 us
    ppermute x1, starting transfers between devices, local(): other = lax.ppermute(found, 'core', [(0, 1), (1, 0)])  4.04 us
  transfers between devices with their start and end apart: 1, of which 1 were waited for; matrix products, arithmetic and copies ran while one was open for 0% of the time, Pallas kernels for 0%

profile of v8, /device:TPU:1, one launch (start us, length us, event | category | flops | bytes accessed | tf_op | source)
XLA Modules:
  0.0 114.9 jit_solution(8735032295580867544)
XLA Ops:
  0.6 1.9 %pack.1 = f32[1344,128]{1,0:T(8,128)} custom-call(s32[1]{0:T(128)} %bitcast.code, f32[2,128,256]{2,1,0:T(8,128)} %mean_all.1, f32[4,2,128,256]{3,2,1,0:T(8,128)} %draws_all.1, s32[2,128]{1,0:T(2,128)} %mask_all.1, f32[2,128]{1,0:T(2,128)} %noise_all.1, f32[2,128]{1,0:T(2,128)} %data_all.1), custom_call_target="tpu_custom_call" | custom-call | tf_op jit(solution)/shard_map/pack/pallas_call | solution.py:323
  2.6 0.0 copy-start
  2.6 55.1 %all_to_all.15 = f32[1344,1,128]{2,1,0:T(1,128)S(1)} all-to-all(f32[1344,1,128]{2,1,0:T(1,128)} %bitcast.15), channel_id=1, replica_groups=mesh['x'=4,'core'=2,'fy'=4,'zq'=4,'zl'=4] {'fy','zq','zl'}, dimensions={0} | all-to-all | bytes 1376256 | tf_op jit(solution)/shard_map/all_to_all | solution.py:340
  57.7 0.0 copy-done
  57.7 1.5 %first.1 = (f32[1,128]{1,0:T(1,128)S(1)}, f32[8,2,64,256]{3,2,1,0:T(8,128)S(1)}, f32[4,2,64,256]{3,2,1,0:T(8,128)S(1)}) custom-call(f32[1344,128]{1,0:T(8,128)S(1)} %bitcast.9, f32[3,256]{1,0:T(4,128)S(1)} %copy-done), custom_call_target="tpu_custom_call" | custom-call | tf_op jit(solution)/shard_map/first/pallas_call | solution.py:344
  59.2 22.1 %all_to_all.16 = f32[128,1,128]{2,1,0:T(1,128)S(1)} all-to-all(f32[128,1,128]{2,1,0:T(1,128)S(1)} %broadcast_in_dim.18), channel_id=1, replica_groups=mesh['x'=4,'core'=2,'fy'=4,'zq'=4,'zl'=4] {'core','x','fy','zl'}, dimensions={0} | all-to-all | bytes 131072 | tf_op jit(solution)/shard_map/all_to_all | solution.py:358
  81.3 1.7 %second.1 = f32[336,128]{1,0:T(8,128)S(1)} custom-call(s32[1]{0:T(128)} %bitcast.code, f32[128,128]{1,0:T(8,128)S(1)} %bitcast.13, f32[1344,128]{1,0:T(8,128)S(1)} %bitcast.10, f32[3,256]{1,0:T(4,128)S(1)} %copy-done, f32[8,2,64,256]{3,2,1,0:T(8,128)S(1)} %get-tuple-element.6.factors, f32[4,2,64,256]{3,2,1,0:T(8,128)S(1)} %get-tuple-element.7.held), custom_call_target="tpu_custom_call" | custom-call | tf_op jit(solution)/shard_map/second/pallas_call | solution.py:361
  83.0 0.1 broadcast_in_dim.20
  83.1 0.1 broadcast_in_dim.21
  83.1 24.8 %all_to_all.17 = f32[1344,1,128]{2,1,0:T(1,128)S(1)} all-to-all(f32[1344,1,128]{2,1,0:T(1,128)S(1)} %bitcast.16), channel_id=1, replica_groups=mesh['x'=4,'core'=2,'fy'=4,'zq'=4,'zl'=4] {'fy','zl','x'}, dimensions={0} | all-to-all | bytes 1376256 | tf_op jit(solution)/shard_map/all_to_all | solution.py:372
  108.0 4.0 %collective-permute-start = (f32[1344,128]{1,0:T(8,128)S(1)}, f32[1344,128]{1,0:T(8,128)S(1)}, u32[]{:S(2)}, u32[]{:S(2)}) collective-permute-start(f32[1344,128]{1,0:T(8,128)S(1)} %bitcast.11), channel_id=1, source_target_pairs={{0,64},{64,0},{1,65},{65,1},{2,66},{66,2},{3,67},{67,3},{4,68},{68... | collective-permute-start | bytes 2064392 | tf_op jit(solution)/shard_map/ppermute | solution.py:374
  112.0 1.7 %collective-permute-done.other = f32[1344,128]{1,0:T(8,128)S(1)} collective-permute-done((f32[1344,128]{1,0:T(8,128)S(1)}, f32[1344,128]{1,0:T(8,128)S(1)}, u32[]{:S(2)}, u32[]{:S(2)}) %collective-permute-start) | collective-permute-done | bytes 688160 | tf_op jit(solution)/shard_map/ppermute | solution.py:374
  113.8 1.2 %last.1 = (f32[2,128,256]{2,1,0:T(8,128)}, f32[2,128,256]{2,1,0:T(8,128)}) custom-call(s32[1]{0:T(128)} %bitcast.code, f32[1344,128]{1,0:T(8,128)S(1)} %bitcast.12, f32[1344,128]{1,0:T(8,128)S(1)} %collective-permute-done.other), custom_call_target="tpu_custom_call" | custom-call | tf_op jit(solution)/shard_map/last/pallas_call | solution.py:376
  (2 shorter events, 0.1 us)
Async XLA Ops:
  2.6 55.1 %copy-start = (f32[3,256]{1,0:T(4,128)S(1)}, f32[3,256]{1,0:T(4,128)}, u32[]{:S(2)}) copy-start(f32[3,256]{1,0:T(4,128)} %kernel.3) | copy-start | bytes 9220
  108.0 5.8 %collective-permute-start = (f32[1344,128]{1,0:T(8,128)S(1)}, f32[1344,128]{1,0:T(8,128)S(1)}, u32[]{:S(2)}, u32[]{:S(2)}) collective-permute-start(f32[1344,128]{1,0:T(8,128)S(1)} %bitcast.11), channel_id=1, source_target_pairs={{0,64},{64,0},{1,65},{65,1},{2,66},{66,2},{3,67},{67,3},{4,68},{68... | collective-permute-start | bytes 2064392 | tf_op jit(solution)/shard_map/ppermute | solution.py:374

commit v9 on v6

--- a/solution.py
+++ b/solution.py
@@ -250,8 +250,9 @@
     for k in range(PAIRS):
         spread = refine(tuple(plane_rows(packed, 1 + k, p, n) for p in range(2)), taps, ends)
         for p in range(2):
-            factors[2 * k, p] = jnp.exp(spread[p])
-            factors[2 * k + 1, p] = jnp.exp(-spread[p])
+            grown = jnp.exp(spread[p])
+            factors[2 * k, p] = grown
+            factors[2 * k + 1, p] = 1.0 / grown
     weight, offset = columns(packed, n)
     basis = krylov(latent, factors, weight, offset, taps, ends)
     for p in range(2):

time: 113 us -> 113 us (level)
  no operation moved by 1% of the time
where the time goes in v9:
time: 113 us
  blocking collectives  98.7 us (87%)
  Pallas kernels  6.24 us (6%)
  starting transfers between devices  5.31 us (5%)
  waiting for transfers between devices  1.75 us (2%)
    all_to_all x1, blocking collectives, local(): lax.all_to_all(packed.reshape(fields * ROWS, 1, 128), ('fy', 'zq', 'zl'),...  55.1 us
    all_to_all x1, blocking collectives, local(): sums = lax.all_to_all(sums, ('core', 'x', 'fy', 'zl'), 0, 0, tiled=True)  22.1 us
    all_to_all x1, blocking collectives, spread(): return lax.all_to_all(block, axis, 0, 0, tiled=True)  11.1 us
    all_to_all x1, blocking collectives, local(): lax.all_to_all(found.reshape(lines * ROWS, 1, 128), ('fy', 'zl'), 0, 0, t...  10.3 us
    ppermute x1, starting transfers between devices, local(): other = lax.ppermute(found, 'core', [(0, 1), (1, 0)])  5.31 us
  transfers between devices with their start and end apart: 1, of which 1 were waited for; matrix products, arithmetic and copies ran while one was open for 0% of the time, Pallas kernels for 0%

profile of v9, /device:TPU:1, one launch (start us, length us, event | category | flops | bytes accessed | tf_op | source)
XLA Modules:
  0.0 112.7 jit_solution(5820514284731815070)
XLA Ops:
  0.6 1.9 %pack.1 = f32[1344,128]{1,0:T(8,128)} custom-call(s32[1]{0:T(128)} %bitcast.code, f32[2,128,256]{2,1,0:T(8,128)} %mean_all.1, f32[4,2,128,256]{3,2,1,0:T(8,128)} %draws_all.1, s32[2,128]{1,0:T(2,128)} %mask_all.1, f32[2,128]{1,0:T(2,128)} %noise_all.1, f32[2,128]{1,0:T(2,128)} %data_all.1), custom_call_target="tpu_custom_call" | custom-call | tf_op jit(solution)/shard_map/pack/pallas_call | solution.py:330
  2.6 0.0 copy-start
  2.6 55.1 %all_to_all.20 = f32[1344,1,128]{2,1,0:T(1,128)S(1)} all-to-all(f32[1344,1,128]{2,1,0:T(1,128)} %bitcast.19), channel_id=1, replica_groups=mesh['x'=4,'core'=2,'fy'=4,'zq'=4,'zl'=4] {'fy','zq','zl'}, dimensions={0} | all-to-all | bytes 1376256 | tf_op jit(solution)/shard_map/all_to_all | solution.py:347
  57.7 0.0 copy-done
  57.7 1.5 %first.1 = (f32[1,128]{1,0:T(1,128)S(1)}, f32[8,2,64,256]{3,2,1,0:T(8,128)S(1)}, f32[4,2,64,256]{3,2,1,0:T(8,128)S(1)}) custom-call(f32[1344,128]{1,0:T(8,128)S(1)} %bitcast.12, f32[3,256]{1,0:T(4,128)S(1)} %copy-done), custom_call_target="tpu_custom_call" | custom-call | tf_op jit(solution)/shard_map/first/pallas_call | solution.py:351
  59.2 22.1 %all_to_all.21 = f32[128,1,128]{2,1,0:T(1,128)S(1)} all-to-all(f32[128,1,128]{2,1,0:T(1,128)S(1)} %broadcast_in_dim.17), channel_id=1, replica_groups=mesh['x'=4,'core'=2,'fy'=4,'zq'=4,'zl'=4] {'core','x','fy','zl'}, dimensions={0} | all-to-all | bytes 131072 | tf_op jit(solution)/shard_map/all_to_all | solution.py:365
  81.3 1.7 %second.1 = f32[336,128]{1,0:T(8,128)S(1)} custom-call(s32[1]{0:T(128)} %bitcast.code, f32[128,128]{1,0:T(8,128)S(1)} %bitcast.17, f32[1344,128]{1,0:T(8,128)S(1)} %bitcast.13, f32[3,256]{1,0:T(4,128)S(1)} %copy-done, f32[8,2,64,256]{3,2,1,0:T(8,128)S(1)} %get-tuple-element.6.factors, f32[4,2,64,256]{3,2,1,0:T(8,128)S(1)} %get-tuple-element.7.held), custom_call_target="tpu_custom_call" | custom-call | tf_op jit(solution)/shard_map/second/pallas_call | solution.py:368
  82.9 10.3 %all_to_all.22 = f32[336,1,128]{2,1,0:T(1,128)S(1)} all-to-all(f32[336,1,128]{2,1,0:T(1,128)S(1)} %bitcast.16), channel_id=1, replica_groups=mesh['x'=4,'core'=2,'fy'=4,'zq'=4,'zl'=4] {'fy','zl'}, dimensions={0} | all-to-all | bytes 344064 | tf_op jit(solution)/shard_map/all_to_all | solution.py:378
  93.3 11.1 %all_to_all.23 = f32[4,336,1,128]{3,1,2,0:T(8,128)S(1)} all-to-all(f32[4,336,1,128]{3,1,2,0:T(8,128)S(1)} %broadcast_in_dim.19), channel_id=1, replica_groups=mesh['x'=4,'core'=2,'fy'=4,'zq'=4,'zl'=4] {'x'}, dimensions={0} | all-to-all | bytes 1376256 | tf_op jit(solution)/shard_map/all_to_all | solution.py:313
  104.5 5.3 %collective-permute-start = (f32[1344,128]{1,0:T(8,128)S(1)}, f32[1344,128]{1,0:T(8,128)S(1)}, u32[]{:S(2)}, u32[]{:S(2)}) collective-permute-start(f32[1344,128]{1,0:T(8,128)S(1)} %bitcast.14), channel_id=1, source_target_pairs={{0,64},{64,0},{1,65},{65,1},{2,66},{66,2},{3,67},{67,3},{4,68},{68... | collective-permute-start | bytes 2064392 | tf_op jit(solution)/shard_map/ppermute | solution.py:380
  109.8 1.7 %collective-permute-done.other = f32[1344,128]{1,0:T(8,128)S(1)} collective-permute-done((f32[1344,128]{1,0:T(8,128)S(1)}, f32[1344,128]{1,0:T(8,128)S(1)}, u32[]{:S(2)}, u32[]{:S(2)}) %collective-permute-start) | collective-permute-done | bytes 688160 | tf_op jit(solution)/shard_map/ppermute | solution.py:380
  111.5 1.2 %last.1 = (f32[2,128,256]{2,1,0:T(8,128)}, f32[2,128,256]{2,1,0:T(8,128)}) custom-call(s32[1]{0:T(128)} %bitcast.code, f32[1344,128]{1,0:T(8,128)S(1)} %bitcast.15, f32[1344,128]{1,0:T(8,128)S(1)} %collective-permute-done.other), custom_call_target="tpu_custom_call" | custom-call | tf_op jit(solution)/shard_map/last/pallas_call | solution.py:382
  (2 shorter events, 0.1 us)
Async XLA Ops:
  2.6 55.1 %copy-start = (f32[3,256]{1,0:T(4,128)S(1)}, f32[3,256]{1,0:T(4,128)}, u32[]{:S(2)}) copy-start(f32[3,256]{1,0:T(4,128)} %kernel.3) | copy-start | bytes 9220
  104.5 7.1 %collective-permute-start = (f32[1344,128]{1,0:T(8,128)S(1)}, f32[1344,128]{1,0:T(8,128)S(1)}, u32[]{:S(2)}, u32[]{:S(2)}) collective-permute-start(f32[1344,128]{1,0:T(8,128)S(1)} %bitcast.14), channel_id=1, source_target_pairs={{0,64},{64,0},{1,65},{65,1},{2,66},{66,2},{3,67},{67,3},{4,68},{68... | collective-permute-start | bytes 2064392 | tf_op jit(solution)/shard_map/ppermute | solution.py:380
